TPU v7x, 128 devices: a whole 4x4x4 slice. The times are simulated.
128 devices in a mesh: ens: 8 (over y_lo, z), grid: 16 (over y_hi, x, core).
Axes of the slice: x: 4, y: 4 (y_hi: 2, y_lo: 2; y = y_hi * 2 + y_lo), z: 4, core: 2. Of those that a mesh axis runs over, the one named last changes fastest.
Arguments:
- latent: bfloat16 [8, 98304, 1024], P('ens', 'grid'), may hold values from -60 to 60
- proj_weight: bfloat16 [1024, 100], replicated, may hold values from -0.1875 to 0.1875
- truth: float32 [100, 98304], P(None, 'grid'), may hold values from -8 to 8
- area_weight: float32 [98304], P('grid'), may hold values from 0.5 to 6
- var_weight: float32 [100], replicated, may hold values from 0.2 to 2
Outputs:
- loss: float32 [], replicated
- latent_grad: bfloat16 [8, 98304, 1024], P('ens', 'grid')
- weight_grad: float32 [1024, 100], P('grid')
All inputs are finite; a program needn't handle non-finite values.
Results may differ from a plain program's by a relative error of at most 0.0087.
The roundings to bfloat16 on the way count: a program that leaves them out, or rounds other values in their place, can miss the bound.
Values may be sent and summed in bfloat16 or wider, within the bound.
A program may use at most 128 MiB of HBM per device.

v0:
```python
import jax
import jax.numpy as jnp
from jax import lax
from jax.sharding import PartitionSpec as P

delta = 0.05


def soft_abs(x):
    return jnp.sqrt(x * x + delta * delta) - delta


def soft_sign(x):
    return x / jnp.sqrt(x * x + delta * delta)


def member_terms(own, stack, target, scale, count):
    skill = soft_abs(own - target)
    spread = jnp.zeros_like(own)
    pulls = jnp.zeros_like(own)
    for other in range(count):
        diff = own - stack[other][None]
        spread = spread + soft_abs(diff)
        pulls = pulls + soft_sign(diff)
    partial_sum = jnp.sum(scale * (skill / count - spread / (2.0 * count * (count - 1))))
    grads = (scale * (soft_sign(own - target) / count - pulls / (count * (count - 1)))).astype(
        jnp.bfloat16
    )
    return (partial_sum, grads)


def per_device(latent, proj_weight, truth, area_weight, var_weight):
    count = lax.axis_size("ens")
    hrows = latent[0]
    local_points = hrows.shape[0]
    preds = lax.dot_general(
        proj_weight, hrows, (((0,), (1,)), ((), ())), preferred_element_type=jnp.float32
    ).astype(jnp.bfloat16)
    sent = preds[None]
    width = local_points // count
    start = lax.axis_index("ens") * width
    scored = lax.all_to_all(sent, "ens", split_axis=2, concat_axis=0, tiled=True).astype(
        jnp.float32
    )
    target = lax.dynamic_slice_in_dim(truth, start, width, 1)[None]
    area_part = lax.dynamic_slice_in_dim(area_weight, start, width, 0)
    scale = (var_weight[:, None] * area_part[None, :])[None]
    partial_sum, block_grads = member_terms(scored, scored, target, scale, count)
    grads = lax.all_to_all(block_grads, "ens", split_axis=0, concat_axis=2, tiled=True)[0]
    total = lax.psum(partial_sum, ("ens", "grid"))
    points_all = local_points * lax.axis_size("grid")
    loss = total / (points_all * truth.shape[0])
    lgrad = lax.dot_general(
        grads, proj_weight, (((0,), (1,)), ((), ())), preferred_element_type=jnp.float32
    )
    latent_grad = lgrad.astype(jnp.bfloat16)[None]
    share_rows = hrows.shape[1] // lax.axis_size("grid")
    wterm = lax.dot_general(
        hrows, grads, (((0,), (1,)), ((), ())), preferred_element_type=jnp.float32
    )
    summed = lax.psum(wterm, ("ens", "grid"))
    mine = lax.dynamic_slice_in_dim(summed, lax.axis_index("grid") * share_rows, share_rows, 0)
    weight_grad = mine / jnp.sqrt(jnp.float32(points_all * count))
    return (loss, latent_grad, weight_grad)


def solution(mesh):
    placed = (P("ens", "grid", None), P(), P(None, "grid"), P("grid"), P())
    return jax.shard_map(
        per_device,
        mesh=mesh,
        in_specs=placed,
        out_specs=(P(), P("ens", "grid", None), P("grid", None)),
        check_vma=False,
    )
```

profile of v0, /device:TPU:1, one launch (start us, length us, event | category | flops | bytes accessed | tf_op | source)
XLA Modules:
  0.0 367.8 jit_solution(7503896122066547778)
XLA Ops:
  7.2 0.9 copy-done
  8.1 9.6 %fusion.7 = bf16[1,100,6144]{2,1,0:T(8,128)(2,1)} fusion(bf16[1024,100]{0,1:T(8,128)(2,1)S(1)} %copy-done, bf16[1,6144,1024]{2,1,0:T(8,128)(2,1)} %param.5), kind=kOutput, calls=%fused_computation.6 | convolution fusion | flops 1258905600 | bytes 14016512 | tf_op jit(solution)/shard_map/dot_general | solution.py:36
  17.7 6.8 %copy.19 = bf16[1,100,6144]{1,0,2:T(2,128)(2,1)S(1)} copy(bf16[1,100,6144]{2,1,0:T(8,128)(2,1)} %fusion.7) | data formatting | bytes 2457600 | tf_op jit(solution)/shard_map/broadcast_in_dim | solution.py:39
  24.5 0.5 broadcast.52
  25.0 34.4 %reduce.2 = bf16[6144,100]{1,0:T(8,128)(2,1)} reduce(bf16[6144,1,100]{2,1,0:T(2,128)(2,1)S(1)} %bitcast.169, bf16[]{:T(256)} %broadcast.52), dimensions={1}, to_apply=%bitcast.160.reduce_sub_computation | reduce | bytes 2457602
  59.5 7.7 %reshape.56 = bf16[8,2,38400]{2,1,0:T(2,128)(2,1)} reshape(bf16[6144,100]{1,0:T(8,128)(2,1)} %reduce.2) | data formatting | bytes 2457600
  67.1 6.9 %all-to-all-start = ((bf16[8,2,38400]{2,1,0:T(2,128)(2,1)}), bf16[8,2,38400]{2,1,0:T(2,128)(2,1)}, u32[]{:S(2)}, u32[]{:S(2)}) async-start(bf16[8,2,38400]{2,1,0:T(2,128)(2,1)} %reshape.56), calls=%async_computation | async-start | bytes 2457600 | tf_op jit(solution)/shard_map/all_to_all | solution.py:42
  74.0 0.8 dynamic_slice.9
  74.8 1.8 broadcast_multiply_fusion
  76.6 14.3 %all-to-all-done = bf16[8,2,38400]{2,1,0:T(2,128)(2,1)} async-done(((bf16[8,2,38400]{2,1,0:T(2,128)(2,1)}), bf16[8,2,38400]{2,1,0:T(2,128)(2,1)}, u32[]{:S(2)}, u32[]{:S(2)}) %all-to-all-start) | async-done | bytes 1228832 | tf_op jit(solution)/shard_map/all_to_all | solution.py:42
  90.9 7.4 %reshape.57 = bf16[6144,1,100]{2,1,0:T(2,128)(2,1)S(1)} reshape(bf16[8,2,38400]{2,1,0:T(2,128)(2,1)} %all-to-all-done) | data formatting | bytes 2457600
  98.4 7.0 %copy.20 = bf16[1,100,6144]{2,0,1:T(2,128)(2,1)} copy(bf16[1,100,6144]{1,0,2:T(2,128)(2,1)S(1)} %bitcast.170) | data formatting | bytes 2457600 | tf_op jit(solution)/shard_map/all_to_all | solution.py:42
  105.4 8.9 %convert_reduce_fusion = f32[100,6144]{1,0:T(8,128)S(1)} fusion(bf16[1,100,6144]{2,0,1:T(2,128)(2,1)} %copy.20), kind=kLoop, calls=%fused_computation.18 | loop fusion | flops 614400 | bytes 3686400 | tf_op jit(solution)/shard_map/convert_element_type | solution.py:42
  114.3 0.8 copy.32
  115.1 0.2 bitcast_bitcast_fusion.1
  115.2 1.7 fusion.22
  117.0 0.1 copy_bitcast_fusion.7
  117.0 0.1 copy_bitcast_fusion.1
  117.2 0.7 copy-done.1
  117.9 0.1 copy-done.2
  118.0 12.3 %multiply_convert_fusion = (bf16[8,100,768]{2,0,1:T(8,128)(2,1)S(1)}, f32[]{:T(128)}) fusion(f32[104,8,768]{2,1,0:T(8,128)S(1)} %bitcast.173, f32[100,768]{1,0:T(8,128)S(1)} %get-tuple-element.28, f32[100,768]{1,0:T(8,128)S(1)} %get-tuple-element.29, f32[100,768]{1,0:T(8,128)S(1)} %get-tuple-element.30, f32[100,768]{1,0:T(8,128)S(1)} %get-tuple-element.31, ...), kind=kLoop, calls=%fused_computation.19 | loop fusion | flops 42393600 | bytes 6758404 | tf_op jit(solution)/shard_map/convert_element_type | solution.py:26
  130.3 1.3 copy.21
  131.6 3.7 %all-to-all-start.1 = ((bf16[8,100,768]{2,1,0:T(8,128)(2,1)}), bf16[8,100,768]{2,1,0:T(8,128)(2,1)S(1)}, u32[]{:S(2)}, u32[]{:S(2)}) async-start(bf16[8,100,768]{2,1,0:T(8,128)(2,1)} %copy.21), calls=%async_computation.1 | async-start | bytes 2555904 | tf_op jit(solution)/shard_map/all_to_all | solution.py:49
  135.4 73.3 %psum.14 = f32[]{:T(128)} all-reduce(f32[]{:T(128)} %get-tuple-element.19), channel_id=1, replica_groups=mesh['ens'=8,'grid'=16] {'ens','grid'}, use_global_device_ids=true, to_apply=%region_1.0 | all-reduce | flops 1 | bytes 8 | tf_op jit(solution)/shard_map/psum | solution.py:50
  209.3 0.2 copy.43
  209.6 0.1 pad
  209.7 0.2 copy.33
  209.9 7.3 %fusion.19 = f32[1024,100]{0,1:T(8,128)} fusion(bf16[100,6144]{1,0:T(8,128)(2,1)S(1)} %bitcast.167, bf16[1,6144,1024]{2,1,0:T(8,128)(2,1)} %param.5), kind=kOutput, calls=%fused_computation.31 | convolution fusion | flops 1258291200 | bytes 14221312 | tf_op jit(solution)/shard_map/dot_general | solution.py:58
  217.2 6.6 %convert_bitcast_fusion = bf16[1,6144,1024]{2,1,0:T(8,128)(2,1)} fusion(bf16[100,6144]{1,0:T(8,128)(2,1)S(1)} %bitcast.168, bf16[1024,100]{0,1:T(8,128)(2,1)S(1)} %copy-done), kind=kOutput, calls=%fused_computation.4 | convolution fusion | flops 1264582656 | bytes 14016512 | tf_op jit(solution)/shard_map/dot_general | solution.py:53
  223.9 134.4 %all-reduce.2.cloned.1.call-done = f32[1024,100]{0,1:T(8,128)} async-done(((f32[1024,100]{0,1:T(8,128)}), f32[1024,100]{0,1:T(8,128)}) %all-reduce.2.cloned.1.call-update) | async-done | bytes 409616 | tf_op jit(solution)/shard_map/psum | solution.py:61
  358.3 0.9 dynamic-slice_multiply_fusion
  359.2 0.7 copy.23
  (10 shorter events, 0.2 us)
Async XLA Ops:
  7.2 0.9 copy-start
  59.5 15.3 %copy-start.3 = (f32[100]{0:T(128)S(1)}, f32[100]{0:T(128)}, u32[]{:S(2)}) copy-start(f32[100]{0:T(128)} %param.9) | copy-start | bytes 1204
  67.1 23.8 %all-to-all-start = ((bf16[8,2,38400]{2,1,0:T(2,128)(2,1)}), bf16[8,2,38400]{2,1,0:T(2,128)(2,1)}, u32[]{:S(2)}, u32[]{:S(2)}) async-start(bf16[8,2,38400]{2,1,0:T(2,128)(2,1)} %reshape.56), calls=%async_computation | async-start | bytes 2457600 | tf_op jit(solution)/shard_map/all_to_all | solution.py:42
  116.9 1.0 copy-start.1
  117.0 1.1 copy-start.2
  131.6 77.7 %all-to-all-start.1 = ((bf16[8,100,768]{2,1,0:T(8,128)(2,1)}), bf16[8,100,768]{2,1,0:T(8,128)(2,1)S(1)}, u32[]{:S(2)}, u32[]{:S(2)}) async-start(bf16[8,100,768]{2,1,0:T(8,128)(2,1)} %copy.21), calls=%async_computation.1 | async-start | bytes 2555904 | tf_op jit(solution)/shard_map/all_to_all | solution.py:49
  135.3 223.0 %all-reduce.2.cloned.1.call-start = ((), (), s32[]{:S(2)}) async-start(), calls=%async_computation.2 | async-start | bytes 851968 | tf_op jit(solution)/shard_map/psum | solution.py:61
Sparse Core Ops, SparseCore 0:
  217.4 140.8 all-reduce.1
where the time goes:
time: 369 us; the launch traced here: 368 us
  waiting for transfers between devices  149 us (40%)
  blocking collectives  73.3 us (20%)
  other arithmetic  58.3 us (16%)
  local copies, waits for them, and re-layouts  37.3 us (10%)
  matrix products  23.6 us (6%)
  between operations  15.9 us (4%)
  starting transfers between devices  10.6 us (3%)
    psum x1, waiting for transfers between devices, per_device(): summed = lax.psum(wterm, ('ens', 'grid'))  134 us
    psum x1, blocking collectives, per_device(): total = lax.psum(partial_sum, ('ens', 'grid'))  73.3 us
    unnamed x1, other arithmetic  34.4 us
    unnamed x19, local copies, waits for them, and re-layouts  19.4 us
    all_to_all x1, waiting for transfers between devices, per_device(): lax.all_to_all(sent, 'ens', split_axis=2, concat_axis=0, tiled=True)  14.3 us
    convert_element_type x1, other arithmetic, member_terms(): (scale * (soft_sign(own - target) / count - pulls / (count * (count - 1))...  12.3 us
    dot_general x1, matrix products, per_device(): lax.dot_general(proj_weight, hrows, (((0,), (1,)), ((), ())), preferred_e...  9.6 us
    convert_element_type x1, other arithmetic, per_device(): lax.all_to_all(sent, 'ens', split_axis=2, concat_axis=0, tiled=True)  8.86 us
  transfers between devices with their start and end apart: 3, of which 2 were waited for; matrix products, arithmetic and copies ran while one was open for 3% of the time, Pallas kernels for 0%

commit v1 on v0

v1 whole, which is shorter than its diff:
```python
import functools
import math

import jax
import jax.numpy as jnp
from jax import lax
from jax.experimental import pallas as pl
from jax.experimental.pallas import tpu as pltpu
from jax.sharding import PartitionSpec as P

DELTA = 0.05
CHUNKS = 3
LANES = 128
ROWS = 16
MESH = pl.DeviceIdType.MESH


def score_block(members, target, scale):
    count = len(members)
    square = DELTA * DELTA
    pulls = [None] * count
    spread = None
    for a in range(count):
        for b in range(a + 1, count):
            diff = members[a] - members[b]
            inner = diff * diff + square
            inverse = lax.rsqrt(inner)
            sign = diff * inverse
            root = inner * inverse
            spread = root if spread is None else spread + root
            pulls[a] = sign if pulls[a] is None else pulls[a] + sign
            pulls[b] = -sign if pulls[b] is None else pulls[b] - sign
    skill = None
    grads = []
    for a in range(count):
        diff = members[a] - target
        inner = diff * diff + square
        inverse = lax.rsqrt(inner)
        root = inner * inverse
        skill = root if skill is None else skill + root
        sign = diff * inverse
        grads.append(scale * (sign * (1.0 / count) - pulls[a] * (1.0 / (count * (count - 1)))))
    crps = skill * (1.0 / count) - spread * (1.0 / (count * (count - 1))) - 0.5 * DELTA
    return scale * crps, grads


def kernel(
    sizes,
    latent_hbm,
    weight_ref,
    truth_hbm,
    area_ref,
    var_ref,
    out_ref,
    wgrad_ref,
    loss_ref,
    latent,
    weight,
    truth,
    var,
    psend,
    precv,
    gsend,
    grecv,
    wsum,
    asend,
    arecv,
    brecv,
    load_sem,
    truth_sem,
    psend_sem,
    precv_sem,
    gsend_sem,
    grecv_sem,
    asend_sem,
    arecv_sem,
    bsend_sem,
    brecv_sem,
):
    count, shards, points, lat, nvar = sizes
    padded = weight.shape[0]
    chunk = points // CHUNKS
    width = chunk // count
    half = count // 2
    me = lax.axis_index("ens")
    mine = lax.axis_index("grid")
    my_y, my_z = me // half, me % half

    def sent_to(slot):
        return ((my_y + slot // half) % 2) * half + (my_z + slot % half) % half

    def came_from(slot):
        return ((my_y + slot // half) % 2) * half + (my_z + half - slot % half) % half

    def load(c):
        rows = pl.ds(c * chunk, chunk)
        return pltpu.make_async_copy(latent_hbm.at[0, rows], latent.at[rows], load_sem.at[c])

    def load_truth(c):
        first = pl.multiple_of(c * chunk + me * width, LANES)
        return pltpu.make_async_copy(truth_hbm.at[:, pl.ds(first, width)], truth.at[c], truth_sem.at[c])

    for c in range(CHUNKS):
        load(c).start()
    for c in range(CHUNKS):
        load_truth(c).start()

    barrier = pltpu.get_barrier_semaphore()
    for slot in range(1, count):
        pl.semaphore_signal(barrier, inc=1, device_id={"ens": sent_to(slot)}, device_id_type=MESH)
    for step in range(1, shards):
        pl.semaphore_signal(barrier, inc=1, device_id={"grid": (mine + step) % shards}, device_id_type=MESH)

    whole = nvar // ROWS * ROWS
    weight[pl.ds(0, whole), :] = weight_ref[pl.ds(0, whole), :]
    weight[pl.ds(whole, padded - whole), :] = jnp.concatenate(
        [
            weight_ref[pl.ds(whole, nvar - whole), :].astype(jnp.float32),
            jnp.zeros((padded - nvar, lat), jnp.float32),
        ],
        axis=0,
    ).astype(jnp.bfloat16)
    row = jnp.concatenate([var_ref[...], jnp.zeros((1, LANES - nvar), jnp.float32)], axis=1)
    var[...] = jnp.broadcast_to(row, (LANES, LANES)).T
    wsum[...] = jnp.zeros_like(wsum)

    pl.semaphore_wait(barrier, count - 1 + shards - 1)

    def send_preds(c, slot):
        return pltpu.make_async_remote_copy(
            src_ref=psend.at[c, slot],
            dst_ref=precv.at[c, slot],
            send_sem=psend_sem.at[c, slot],
            recv_sem=precv_sem.at[c, slot],
            device_id={"ens": sent_to(slot)},
            device_id_type=MESH,
        )

    def send_grads(c, slot):
        lanes = pl.ds(pl.multiple_of(me * width, LANES), width)
        return pltpu.make_async_remote_copy(
            src_ref=gsend.at[c, slot],
            dst_ref=grecv.at[c, :, lanes],
            send_sem=gsend_sem.at[c, slot],
            recv_sem=grecv_sem.at[c, slot],
            device_id={"ens": came_from(slot)},
            device_id_type=MESH,
        )

    def project(c, slot):
        first = pl.multiple_of(c * chunk + sent_to(slot) * width, LANES)
        return lax.dot_general(
            weight[...],
            latent[pl.ds(first, width), :],
            (((1,), (1,)), ((), ())),
            preferred_element_type=jnp.float32,
        ).astype(jnp.bfloat16)

    for c in range(CHUNKS):
        load(c).wait()

        def forward(step, carry, c=c):
            slot = count - 1 - step
            psend[c, slot] = project(c, slot)
            send_preds(c, slot).start()
            return carry

        lax.fori_loop(0, count - 1, forward, 0)
        precv[c, 0] = project(c, 0)

    total = jnp.zeros((8, LANES), jnp.float32)
    blocks = width // LANES
    for c in range(CHUNKS):
        load_truth(c).wait()
        for slot in range(1, count):
            send_preds(c, slot).wait_recv()
        first = (c * chunk + me * width) // LANES

        def put(slot, rows, lane, value, c=c):
            if slot == 0:
                lanes = pl.ds(pl.multiple_of(me * width + lane, LANES), LANES)
                grecv[c, rows, lanes] = value
            else:
                gsend[c, slot, rows, pl.ds(lane, LANES)] = value

        def whole_rows(step, acc, c=c, first=first):
            block = step % blocks
            lane = pl.multiple_of(block * LANES, LANES)
            start = pl.multiple_of(step // blocks * ROWS, ROWS)
            rows = pl.ds(start, ROWS)
            members = [precv[c, s, rows, pl.ds(lane, LANES)].astype(jnp.float32) for s in range(count)]
            target = truth[c, rows, pl.ds(lane, LANES)]
            scale = var[rows, :] * area_ref[pl.ds(first + block, 1), :]
            terms, grads = score_block(members, target, scale)
            for s in range(count):
                put(s, rows, lane, grads[s].astype(jnp.bfloat16))
            return acc + terms[:8] + terms[8:]

        total = lax.fori_loop(0, whole // ROWS * blocks, whole_rows, total)

        def last_rows(block, acc, c=c, first=first):
            lane = pl.multiple_of(block * LANES, LANES)
            rows = pl.ds(whole, ROWS)
            members = [precv[c, s, rows, pl.ds(lane, LANES)].astype(jnp.float32)[:8] for s in range(count)]
            target = jnp.concatenate(
                [truth[c, pl.ds(whole, nvar - whole), pl.ds(lane, LANES)], jnp.zeros((8 - nvar + whole, LANES), jnp.float32)],
                axis=0,
            )
            scale = var[pl.ds(whole, 8), :] * area_ref[pl.ds(first + block, 1), :]
            terms, grads = score_block(members, target, scale)
            rest = jnp.zeros((ROWS - 8, LANES), jnp.float32)
            for s in range(count):
                put(s, rows, lane, jnp.concatenate([grads[s], rest], axis=0).astype(jnp.bfloat16))
            return acc + terms

        total = lax.fori_loop(0, blocks, last_rows, total)
        for slot in range(count - 1, 0, -1):
            send_grads(c, slot).start()
    partial = jnp.sum(total)

    cut = 256
    for c in range(CHUNKS):
        for slot in range(1, count):
            send_grads(c, slot).wait_recv()

        def weight_part(step, carry, c=c):
            lanes = pl.ds(pl.multiple_of(step * cut, cut), cut)
            wsum[pl.ds(0, padded), lanes] += jnp.dot(
                grecv[c], latent[pl.ds(c * chunk, chunk), lanes], preferred_element_type=jnp.float32
            )
            return carry

        lax.fori_loop(0, lat // cut, weight_part, 0)
        if c == CHUNKS - 1:
            wsum[pl.ds(padded, LANES - padded), :] = jnp.broadcast_to(partial, (LANES - padded, lat))
            share = lat // shards
            for block in range(lat // LANES):
                turned = wsum[:, pl.ds(block * LANES, LANES)].T
                for part in range(LANES // share):
                    asend[block * (LANES // share) + part] = turned[part * share : (part + 1) * share]
            arecv[mine] = asend[mine]
            for step in range(1, shards):
                send_share(asend, arecv, asend_sem, arecv_sem, mine, shards, step).start()

        def latent_part(step, carry, c=c):
            lanes = pl.ds(pl.multiple_of(step * cut, cut), cut)
            rows = pl.ds(pl.multiple_of(c * chunk + step * cut, cut), cut)
            out_ref[0, rows, :] = lax.dot_general(
                grecv[c, :, lanes], weight[...], (((0,), (0,)), ((), ())), preferred_element_type=jnp.float32
            ).astype(jnp.bfloat16)
            return carry

        lax.fori_loop(0, chunk // cut, latent_part, 0)

    for step in range(1, shards):
        send_share(asend, arecv, asend_sem, arecv_sem, mine, shards, step).wait_recv()
    summed = arecv[0]
    for k in range(1, shards):
        summed = summed + arecv[k]
    brecv[me] = summed
    for slot in range(1, count):
        send_sum(brecv, bsend_sem, brecv_sem, me, sent_to, slot).start()
    for slot in range(1, count):
        send_sum(brecv, bsend_sem, brecv_sem, me, sent_to, slot).wait_recv()
    final = brecv[0]
    for k in range(1, count):
        final = final + brecv[k]
    wgrad_ref[...] = final[:, :nvar] * (1.0 / math.sqrt(points * shards * count))
    loss_ref[...] = final[0:1, LANES - 1 : LANES] * (1.0 / (points * shards * nvar))

    for c in range(CHUNKS):
        for slot in range(1, count):
            send_preds(c, slot).wait_send()
            send_grads(c, slot).wait_send()
    for step in range(1, shards):
        send_share(asend, arecv, asend_sem, arecv_sem, mine, shards, step).wait_send()
    for slot in range(1, count):
        send_sum(brecv, bsend_sem, brecv_sem, me, sent_to, slot).wait_send()


def send_share(asend, arecv, send_sem, recv_sem, mine, shards, step):
    to = (mine + step) % shards
    return pltpu.make_async_remote_copy(
        src_ref=asend.at[to],
        dst_ref=arecv.at[mine],
        send_sem=send_sem.at[step],
        recv_sem=recv_sem.at[step],
        device_id={"grid": to},
        device_id_type=MESH,
    )


def send_sum(brecv, send_sem, recv_sem, me, sent_to, slot):
    return pltpu.make_async_remote_copy(
        src_ref=brecv.at[me],
        dst_ref=brecv.at[me],
        send_sem=send_sem.at[slot],
        recv_sem=recv_sem.at[slot],
        device_id={"ens": sent_to(slot)},
        device_id_type=MESH,
    )


def per_device(latent, proj_weight, truth, area_weight, var_weight):
    count, shards = lax.axis_size("ens"), lax.axis_size("grid")
    _, points, lat = latent.shape
    nvar = truth.shape[0]
    padded = -(-nvar // ROWS) * ROWS
    width = points // CHUNKS // count
    share = lat // shards
    sizes = (count, shards, points, lat, nvar)
    hbm = pl.BlockSpec(memory_space=pl.ANY)
    vmem = pl.BlockSpec(memory_space=pltpu.VMEM)
    dma = pltpu.SemaphoreType.DMA
    latent_grad, weight_grad, loss = pl.pallas_call(
        functools.partial(kernel, sizes),
        out_shape=(
            jax.ShapeDtypeStruct((1, points, lat), jnp.bfloat16),
            jax.ShapeDtypeStruct((share, nvar), jnp.float32),
            jax.ShapeDtypeStruct((1, 1), jnp.float32),
        ),
        in_specs=[hbm, vmem, hbm, vmem, vmem],
        out_specs=(vmem, vmem, vmem),
        scratch_shapes=[
            pltpu.VMEM((points, lat), jnp.bfloat16),
            pltpu.VMEM((padded, lat), jnp.bfloat16),
            pltpu.VMEM((CHUNKS, nvar, width), jnp.float32),
            pltpu.VMEM((LANES, LANES), jnp.float32),
            pltpu.VMEM((CHUNKS, count, padded, width), jnp.bfloat16),
            pltpu.VMEM((CHUNKS, count, padded, width), jnp.bfloat16),
            pltpu.VMEM((CHUNKS, count, padded, width), jnp.bfloat16),
            pltpu.VMEM((CHUNKS, padded, points // CHUNKS), jnp.bfloat16),
            pltpu.VMEM((LANES, lat), jnp.float32),
            pltpu.VMEM((shards, share, LANES), jnp.float32),
            pltpu.VMEM((shards, share, LANES), jnp.float32),
            pltpu.VMEM((count, share, LANES), jnp.float32),
            dma((CHUNKS,)),
            dma((CHUNKS,)),
            dma((CHUNKS, count)),
            dma((CHUNKS, count)),
            dma((CHUNKS, count)),
            dma((CHUNKS, count)),
            dma((shards,)),
            dma((shards,)),
            dma((count,)),
            dma((count,)),
        ],
        compiler_params=pltpu.CompilerParams(
            collective_id=0, has_side_effects=True, vmem_limit_bytes=48 * 2**20
        ),
        name="crps_step",
    )(
        latent,
        proj_weight.T,
        truth,
        area_weight.reshape(points // LANES, LANES),
        var_weight.reshape(1, nvar),
    )
    return (loss[0, 0], latent_grad, weight_grad)


def solution(mesh):
    placed = (P("ens", "grid", None), P(), P(None, "grid"), P("grid"), P())
    return jax.shard_map(
        per_device,
        mesh=mesh,
        in_specs=placed,
        out_specs=(P(), P("ens", "grid", None), P("grid", None)),
        check_vma=False,
    )
```

time: 369 us -> 80.1 us (0.22)
  waiting for transfers between devices: 149 us -> 0 us
  blocking collectives: 73.3 us -> 0 us
  Pallas kernels: 0 us -> 62.1 us
  other arithmetic: 58.3 us -> 0 us
  matrix products: 23.6 us -> 0 us
  local copies, waits for them, and re-layouts: 37.3 us -> 15.2 us
  between operations: 15.9 us -> 2.4 us
  starting transfers between devices: 10.6 us -> 0 us
    psum x1 -> x0, waiting for transfers between devices: 134 us -> none  [per_device(): summed = lax.psum(wterm, ('ens', 'grid'))]
    psum x1 -> x0, blocking collectives: 73.3 us -> none  [per_device(): total = lax.psum(partial_sum, ('ens', 'grid'))]
    pallas_call x0 -> x1, Pallas kernels: none -> 62.1 us  [per_device(): pl.pallas_call(functools.partial(kernel, sizes), out_shape=(jax.ShapeDtyp...]
    unnamed x1 -> x0, other arithmetic: 34.4 us -> none
    dot_general x3 -> x0, matrix products: 23.6 us -> none  [the longest x1 9.6 us: per_device(): lax.dot_general(proj_weight, hrows, (((0,), (1,)), ((), ())), preferred_e...]
    convert_element_type x2 -> x0, other arithmetic: 21.2 us -> none  [the longest x1 12.3 us: member_terms(): (scale * (soft_sign(own - target) / count - pulls / (count * (count - 1))...]
    all_to_all x2 -> x0, waiting for transfers between devices: 14.4 us -> none  [the longest x1 14.3 us: per_device(): lax.all_to_all(sent, 'ens', split_axis=2, concat_axis=0, tiled=True)]
    all_to_all x2 -> x0, starting transfers between devices: 10.6 us -> none  [the longest x1 6.88 us: per_device(): lax.all_to_all(sent, 'ens', split_axis=2, concat_axis=0, tiled=True)]
  transfers between devices with their start and end apart: 3 -> 0, of which waited for: 2 -> 0; matrix products, arithmetic and copies ran while one was open for 3% -> 0% of each run, Pallas kernels for 0% -> 0%
where the time goes in v1:
time: 80.1 us; the launch traced here: 79.7 us
  Pallas kernels  62.1 us (78%)
  local copies, waits for them, and re-layouts  15.2 us (19%)
  between operations  2.4 us (3%)
    pallas_call x1, Pallas kernels, per_device(): pl.pallas_call(functools.partial(kernel, sizes), out_shape=(jax.ShapeDtyp...  62.1 us
    unnamed x10, local copies, waits for them, and re-layouts  15.2 us

profile of v1, /device:TPU:1, one launch (start us, length us, event | category | flops | bytes accessed | tf_op | source)
XLA Modules:
  0.0 79.7 jit_solution(16525580341594418481)
XLA Ops:
  0.6 0.0 copy-start
  0.6 1.7 %copy-done = f32[100,6144]{1,0:T(8,128)S(1)} copy-done((f32[100,6144]{1,0:T(8,128)S(1)}, f32[100,6144]{1,0:T(8,128)}, u32[]{:S(2)}) %copy-start) | copy-done | bytes 2457624
  2.4 0.0 copy-start.1
  2.4 0.9 %copy-done.1 = bf16[1024,100]{0,1:T(8,128)(2,1)S(1)} copy-done((bf16[1024,100]{0,1:T(8,128)(2,1)S(1)}, bf16[1024,100]{0,1:T(8,128)(2,1)}, u32[]{:S(2)}) %copy-start.1) | copy-done | bytes 204824
  3.3 0.0 copy-start.2
  3.3 0.7 copy-done.2
  4.0 0.0 copy-start.3
  4.0 0.7 copy-done.3
  4.7 62.1 %crps_step.1 = (bf16[1,6144,1024]{2,1,0:T(8,128)(2,1)}, f32[64,100]{1,0:T(8,128)S(1)}, f32[1,1]{1,0:T(1,128)}) custom-call(bf16[1,6144,1024]{2,1,0:T(8,128)(2,1)} %latent_hbm.1, bf16[100,1024]{1,0:T(8,128)(2,1)S(1)} %bitcast.4, f32[100,6144]{1,0:T(8,128)S(1)} %copy-done, f32[48,128]{1,0:T(8,128)S(1)} %bitcast.5, f32[1,100]{1,0:T(1,128)S(1)} %bitcast.6), custom_call_target="tpu_custom_call" | custom-call | tf_op jit(solution)/shard_map/crps_step/pallas_call | solution.py:315
  67.4 10.5 %copy.12 = bf16[1,6144,1024]{2,1,0:T(8,128)(2,1)} copy(bf16[1,6144,1024]{2,1,0:T(8,128)(2,1)} %get-tuple-element.13) | data formatting | bytes 25165824
  78.0 0.6 copy.13
Async XLA Ops:
  0.6 1.7 %copy-start = (f32[100,6144]{1,0:T(8,128)S(1)}, f32[100,6144]{1,0:T(8,128)}, u32[]{:S(2)}) copy-start(f32[100,6144]{1,0:T(8,128)} %truth_hbm.1) | copy-start | bytes 7372804
  2.4 0.9 %copy-start.1 = (bf16[1024,100]{0,1:T(8,128)(2,1)S(1)}, bf16[1024,100]{0,1:T(8,128)(2,1)}, u32[]{:S(2)}) copy-start(bf16[1024,100]{0,1:T(8,128)(2,1)} %param.6) | copy-start | bytes 614404
  3.3 0.7 copy-start.2
  4.0 0.7 copy-start.3

commit v2 on v1

v2 whole, which is shorter than its diff:
```python
import functools
import math

import jax
import jax.numpy as jnp
from jax import lax
from jax.experimental import pallas as pl
from jax.experimental.pallas import tpu as pltpu
from jax.sharding import PartitionSpec as P

DELTA = 0.05
CHUNKS = 3
LANES = 128
ROWS = 16
MESH = pl.DeviceIdType.MESH


def score_block(members, target, scale):
    count = len(members)
    square = DELTA * DELTA
    pulls = [None] * count
    spread = None
    for a in range(count):
        for b in range(a + 1, count):
            diff = members[a] - members[b]
            inner = diff * diff + square
            inverse = lax.rsqrt(inner)
            sign = diff * inverse
            root = inner * inverse
            spread = root if spread is None else spread + root
            pulls[a] = sign if pulls[a] is None else pulls[a] + sign
            pulls[b] = -sign if pulls[b] is None else pulls[b] - sign
    skill = None
    grads = []
    for a in range(count):
        diff = members[a] - target
        inner = diff * diff + square
        inverse = lax.rsqrt(inner)
        root = inner * inverse
        skill = root if skill is None else skill + root
        sign = diff * inverse
        grads.append(scale * (sign * (1.0 / count) - pulls[a] * (1.0 / (count * (count - 1)))))
    crps = skill * (1.0 / count) - spread * (1.0 / (count * (count - 1))) - 0.5 * DELTA
    return scale * crps, grads


def kernel(
    sizes,
    latent_hbm,
    weight_hbm,
    truth_hbm,
    area_hbm,
    var_hbm,
    out_ref,
    wgrad_ref,
    loss_ref,
    latent,
    weight_in,
    weight,
    truth,
    area,
    var_in,
    var,
    psend,
    precv,
    gsend,
    grecv,
    grads,
    wsum,
    asend,
    arecv,
    bsend,
    brecv,
    crecv,
    load_sem,
    truth_sem,
    small_sem,
    psend_sem,
    precv_sem,
    gsend_sem,
    grecv_sem,
    asend_sem,
    arecv_sem,
    bsend_sem,
    brecv_sem,
    csend_sem,
    crecv_sem,
):
    count, shards, points, lat, nvar = sizes
    padded = weight.shape[0]
    chunk = points // CHUNKS
    width = chunk // count
    blocks = width // LANES
    half = count // 2
    whole = nvar // ROWS * ROWS
    left = nvar - whole
    tail = blocks * whole
    me = lax.axis_index("ens")
    mine = lax.axis_index("grid")
    my_y, my_z = me // half, me % half
    core, spot = mine % 2, mine // 2
    spots = shards // 2
    place = my_y * spots + spot
    places = 2 * spots

    def sent_to(slot):
        return ((my_y + slot // half) % 2) * half + (my_z + slot % half) % half

    def came_from(slot):
        return ((my_y + slot // half) % 2) * half + (my_z + half - slot % half) % half

    def device_at(there):
        return {"ens": there // spots * half + my_z, "grid": there % spots * 2 + core}

    def load(c):
        rows = pl.ds(c * chunk, chunk)
        return pltpu.make_async_copy(latent_hbm.at[0, rows], latent.at[rows], load_sem.at[c])

    def load_truth(c):
        first = pl.multiple_of(c * chunk + me * width, LANES)
        return pltpu.make_async_copy(truth_hbm.at[:, pl.ds(first, width)], truth.at[c], truth_sem.at[c])

    small = [
        pltpu.make_async_copy(weight_hbm, weight_in, small_sem.at[0]),
        pltpu.make_async_copy(var_hbm, var_in, small_sem.at[1]),
        pltpu.make_async_copy(area_hbm, area, small_sem.at[2]),
    ]
    for copy in small:
        copy.start()
    for c in range(CHUNKS):
        load(c).start()
    for c in range(CHUNKS):
        load_truth(c).start()

    sibling = mine + 1 - 2 * core
    barrier = pltpu.get_barrier_semaphore()
    for slot in range(1, count):
        pl.semaphore_signal(barrier, inc=1, device_id={"ens": sent_to(slot)}, device_id_type=MESH)
    for step in range(1, places):
        pl.semaphore_signal(barrier, inc=1, device_id=device_at((place + step) % places), device_id_type=MESH)
    pl.semaphore_signal(barrier, inc=1, device_id={"grid": sibling}, device_id_type=MESH)

    for copy in small:
        copy.wait()
    weight[pl.ds(0, whole), :] = weight_in[pl.ds(0, whole), :]
    weight[pl.ds(whole, padded - whole), :] = jnp.concatenate(
        [
            weight_in[pl.ds(whole, left), :].astype(jnp.float32),
            jnp.zeros((padded - nvar, lat), jnp.float32),
        ],
        axis=0,
    ).astype(jnp.bfloat16)
    row = jnp.concatenate([var_in[...], jnp.zeros((1, LANES - nvar), jnp.float32)], axis=1)
    var[...] = jnp.broadcast_to(row, (LANES, LANES)).T

    def send_preds(c, slot):
        return pltpu.make_async_remote_copy(
            src_ref=psend.at[c, slot],
            dst_ref=precv.at[c, slot],
            send_sem=psend_sem.at[c, slot],
            recv_sem=precv_sem.at[c, slot],
            device_id={"ens": sent_to(slot)},
            device_id_type=MESH,
        )

    def send_grads(c, slot):
        return pltpu.make_async_remote_copy(
            src_ref=gsend.at[c, slot],
            dst_ref=grecv.at[c, slot],
            send_sem=gsend_sem.at[c, slot],
            recv_sem=grecv_sem.at[c, slot],
            device_id={"ens": came_from(slot)},
            device_id_type=MESH,
        )

    def send_core(step):
        some = pl.ds(step * 2, 2)
        return pltpu.make_async_remote_copy(
            src_ref=asend.at[1 - core, some],
            dst_ref=arecv.at[some],
            send_sem=asend_sem.at[step],
            recv_sem=arecv_sem.at[step],
            device_id={"grid": sibling},
            device_id_type=MESH,
        )

    def send_share(step):
        there = (place + step) % places
        rows = pl.ds(pl.multiple_of(there // spots * brecv.shape[1], 8), brecv.shape[1])
        return pltpu.make_async_remote_copy(
            src_ref=bsend.at[there % spots, rows],
            dst_ref=brecv.at[place],
            send_sem=bsend_sem.at[step],
            recv_sem=brecv_sem.at[step],
            device_id=device_at(there),
            device_id_type=MESH,
        )

    def send_sum(slot):
        return pltpu.make_async_remote_copy(
            src_ref=crecv.at[me],
            dst_ref=crecv.at[me],
            send_sem=csend_sem.at[slot],
            recv_sem=crecv_sem.at[slot],
            device_id={"ens": sent_to(slot)},
            device_id_type=MESH,
        )

    def project(target, c, slot):
        first = pl.multiple_of(c * chunk + sent_to(slot) * width, LANES)
        preds = lax.dot_general(
            weight[...],
            latent[pl.ds(first, width), :],
            (((1,), (1,)), ((), ())),
            preferred_element_type=jnp.float32,
        )
        for b in range(blocks):
            target[c, slot, pl.ds(b * whole, whole), :] = preds[:whole, b * LANES : (b + 1) * LANES].astype(jnp.bfloat16)
        rest = [preds[whole:nvar, b * LANES : (b + 1) * LANES] for b in range(blocks)]
        rest.append(jnp.zeros((ROWS - blocks * left, LANES), jnp.float32))
        target[c, slot, pl.ds(tail, ROWS), :] = jnp.concatenate(rest, axis=0).astype(jnp.bfloat16)

    for c in range(CHUNKS):
        load(c).wait()

        def forward(step, carry, c=c):
            slot = count - 1 - step
            project(psend, c, slot)
            if c == 0:

                @pl.when(step == 0)
                def _():
                    pl.semaphore_wait(barrier, count - 1 + places - 1 + 1)

            send_preds(c, slot).start()
            return carry

        lax.fori_loop(0, count - 1, forward, 0)
        project(precv, c, 0)

    total = jnp.zeros((8, LANES), jnp.float32)
    for c in range(CHUNKS):
        load_truth(c).wait()
        for slot in range(1, count):
            send_preds(c, slot).wait_recv()
        first = (c * chunk + me * width) // LANES

        def put(rows, values, c=c):
            grecv[c, 0, rows, :] = values[0].astype(jnp.bfloat16)
            for s in range(1, count):
                gsend[c, s, rows, :] = values[s].astype(jnp.bfloat16)

        def whole_rows(step, acc, c=c, first=first, put=put):
            block = step % blocks
            lanes = pl.ds(pl.multiple_of(block * LANES, LANES), LANES)
            start = pl.multiple_of(step // blocks * ROWS, ROWS)
            rows = pl.ds(pl.multiple_of(block * whole + start, ROWS), ROWS)
            members = [precv[c, s, rows, :].astype(jnp.float32) for s in range(count)]
            target = truth[c, pl.ds(start, ROWS), lanes]
            scale = var[pl.ds(start, ROWS), :] * area[pl.ds(first + block, 1), :]
            terms, pulled = score_block(members, target, scale)
            put(rows, pulled)
            return acc + terms[:8] + terms[8:]

        total = lax.fori_loop(0, whole // ROWS * blocks, whole_rows, total)

        rows = pl.ds(tail, ROWS)
        members = [precv[c, s, rows, :].astype(jnp.float32)[:8] for s in range(count)]
        spare = [jnp.zeros((8 - blocks * left, LANES), jnp.float32)] if blocks * left < 8 else []
        target = jnp.concatenate(
            [truth[c, pl.ds(whole, left), pl.ds(b * LANES, LANES)] for b in range(blocks)] + spare, axis=0
        )
        scale = jnp.concatenate(
            [var[pl.ds(whole, left), :] * area[pl.ds(first + b, 1), :] for b in range(blocks)] + spare, axis=0
        )
        terms, pulled = score_block(members, target, scale)
        rest = jnp.zeros((ROWS - 8, LANES), jnp.float32)
        put(rows, [jnp.concatenate([value, rest], axis=0) for value in pulled])
        total = total + terms
        for slot in range(count - 1, 0, -1):
            send_grads(c, slot).start()
    partial = jnp.sum(total)

    cut = 256

    def weight_part(step, c):
        lanes = pl.ds(pl.multiple_of(step * cut, cut), cut)
        part = jnp.dot(grads[...], latent[pl.ds(c * chunk, chunk), lanes], preferred_element_type=jnp.float32)
        if c == 0:
            wsum[pl.ds(0, padded), lanes] = part
        else:
            wsum[pl.ds(0, padded), lanes] += part

    def latent_part(step, c):
        lanes = pl.ds(pl.multiple_of(step * cut, cut), cut)
        rows = pl.ds(pl.multiple_of(c * chunk + step * cut, cut), cut)
        out_ref[0, rows, :] = lax.dot_general(
            grads[:, lanes], weight[...], (((0,), (0,)), ((), ())), preferred_element_type=jnp.float32
        ).astype(jnp.bfloat16)

    def loop(start, stop, body):
        def step_of(step, carry):
            body(step)
            return carry

        lax.fori_loop(start, stop, step_of, 0)

    for c in range(CHUNKS):
        for slot in range(1, count):
            send_grads(c, slot).wait_recv()

        def unpack(slot, c=c):
            at = sent_to(slot) * width
            last = grecv[c, slot, pl.ds(tail, ROWS), :].astype(jnp.float32)
            for b in range(blocks):
                lanes = pl.ds(pl.multiple_of(at + b * LANES, LANES), LANES)
                grads[pl.ds(0, whole), lanes] = grecv[c, slot, pl.ds(b * whole, whole), :]
                grads[pl.ds(whole, ROWS), lanes] = jnp.concatenate(
                    [last[b * left : (b + 1) * left], jnp.zeros((ROWS - left, LANES), jnp.float32)], axis=0
                ).astype(jnp.bfloat16)

        loop(0, count, unpack)
        if c < CHUNKS - 1:
            loop(0, lat // cut, lambda step, c=c: weight_part(step, c))
            loop(0, chunk // cut, lambda step, c=c: latent_part(step, c))

    c = CHUNKS - 1
    wsum[pl.ds(padded, LANES - padded), :] = jnp.broadcast_to(partial, (LANES - padded, lat))

    def weight_sent(step):
        weight_part(step, c)
        for b in range(cut // LANES):
            lanes = pl.ds(pl.multiple_of(step * cut + b * LANES, LANES), LANES)
            turned = wsum[:, lanes].T
            asend[0, step * 2 + b] = turned[: LANES // 2]
            asend[1, step * 2 + b] = turned[LANES // 2 :]
        send_core(step).start()

    loop(0, lat // cut, weight_sent)
    early = 2
    loop(0, early, lambda step: latent_part(step, c))
    for step in range(lat // cut):
        send_core(step).wait_recv()
    bsend[...] = asend[core] + arecv[...]
    for step in range(1, places):
        send_share(step).start()
    brecv[place] = bsend[spot, pl.ds(pl.multiple_of(my_y * brecv.shape[1], 8), brecv.shape[1]), :]
    loop(early, chunk // cut, lambda step: latent_part(step, c))
    for step in range(1, places):
        send_share(step).wait_recv()
    summed = brecv[0]
    for k in range(1, places):
        summed = summed + brecv[k]
    crecv[me] = summed
    for slot in range(1, count):
        send_sum(slot).start()
    for slot in range(1, count):
        send_sum(slot).wait_recv()
    for y in range(2):
        final = crecv[y * half]
        for k in range(1, half):
            final = final + crecv[y * half + k]
        rows = pl.ds(y * brecv.shape[1], brecv.shape[1])
        wgrad_ref[rows, :] = final[:, :nvar] * (1.0 / math.sqrt(points * shards * count))
        if y == 0:
            loss_ref[...] = final[0:1, LANES - 1 : LANES] * (1.0 / (points * shards * nvar))

    for c in range(CHUNKS):
        for slot in range(1, count):
            send_preds(c, slot).wait_send()
            send_grads(c, slot).wait_send()
    for step in range(lat // cut):
        send_core(step).wait_send()
    for step in range(1, places):
        send_share(step).wait_send()
    for slot in range(1, count):
        send_sum(slot).wait_send()


def copy_out(latent_grad, wgrad, loss, latent_out, wgrad_out, loss_out, sem):
    copy = pltpu.make_async_copy(latent_grad, latent_out, sem)
    copy.start()
    wgrad_out[...] = wgrad[...]
    loss_out[...] = loss[...]
    copy.wait()


def per_device(latent, proj_weight, truth, area_weight, var_weight):
    count, shards = lax.axis_size("ens"), lax.axis_size("grid")
    _, points, lat = latent.shape
    nvar = truth.shape[0]
    padded = -(-nvar // ROWS) * ROWS
    width = points // CHUNKS // count
    packed = width // LANES * (nvar // ROWS * ROWS) + ROWS
    share = lat // shards
    sizes = (count, shards, points, lat, nvar)
    hbm = pl.BlockSpec(memory_space=pltpu.HBM)
    vmem = pl.BlockSpec(memory_space=pltpu.VMEM)
    dma = pltpu.SemaphoreType.DMA
    out_shape = (
        jax.ShapeDtypeStruct((1, points, lat), jnp.bfloat16),
        jax.ShapeDtypeStruct((share, nvar), jnp.float32),
        jax.ShapeDtypeStruct((1, 1), jnp.float32),
    )
    results = pl.pallas_call(
        functools.partial(kernel, sizes),
        out_shape=(pltpu.VMEM((1, points, lat), jnp.bfloat16), *out_shape[1:]),
        in_specs=[hbm] * 5,
        out_specs=(vmem, vmem, vmem),
        scratch_shapes=[
            pltpu.VMEM((points, lat), jnp.bfloat16),
            pltpu.VMEM((nvar, lat), jnp.bfloat16),
            pltpu.VMEM((padded, lat), jnp.bfloat16),
            pltpu.VMEM((CHUNKS, nvar, width), jnp.float32),
            pltpu.VMEM((points // LANES, LANES), jnp.float32),
            pltpu.VMEM((1, nvar), jnp.float32),
            pltpu.VMEM((LANES, LANES), jnp.float32),
            pltpu.VMEM((CHUNKS, count, packed, LANES), jnp.bfloat16),
            pltpu.VMEM((CHUNKS, count, packed, LANES), jnp.bfloat16),
            pltpu.VMEM((CHUNKS, count, packed, LANES), jnp.bfloat16),
            pltpu.VMEM((CHUNKS, count, packed, LANES), jnp.bfloat16),
            pltpu.VMEM((padded, points // CHUNKS), jnp.bfloat16),
            pltpu.VMEM((LANES, lat), jnp.float32),
            pltpu.VMEM((2, shards // 2, share, LANES), jnp.float32),
            pltpu.VMEM((shards // 2, share, LANES), jnp.float32),
            pltpu.VMEM((shards // 2, share, LANES), jnp.float32),
            pltpu.VMEM((shards, share // 2, LANES), jnp.float32),
            pltpu.VMEM((count, share // 2, LANES), jnp.float32),
            dma((CHUNKS,)),
            dma((CHUNKS,)),
            dma((3,)),
            dma((CHUNKS, count)),
            dma((CHUNKS, count)),
            dma((CHUNKS, count)),
            dma((CHUNKS, count)),
            dma((lat // 256,)),
            dma((lat // 256,)),
            dma((shards,)),
            dma((shards,)),
            dma((count,)),
            dma((count,)),
        ],
        compiler_params=pltpu.CompilerParams(
            collective_id=0, has_side_effects=True, vmem_limit_bytes=36 * 2**20
        ),
        name="crps_step",
    )(
        *(
            pltpu.with_memory_space_constraint(x, pltpu.HBM)
            for x in (
                latent,
                proj_weight.T,
                truth,
                area_weight.reshape(points // LANES, LANES),
                var_weight.reshape(1, nvar),
            )
        )
    )
    latent_grad, weight_grad, loss = pl.pallas_call(
        copy_out,
        out_shape=out_shape,
        in_specs=[vmem, vmem, vmem],
        out_specs=(hbm, vmem, vmem),
        scratch_shapes=[dma],
        compiler_params=pltpu.CompilerParams(vmem_limit_bytes=2**20),
        name="copy_out",
    )(pltpu.with_memory_space_constraint(results[0], pltpu.VMEM), *results[1:])
    return (loss[0, 0], latent_grad, weight_grad)


def solution(mesh):
    placed = (P("ens", "grid", None), P(), P(None, "grid"), P("grid"), P())
    return jax.shard_map(
        per_device,
        mesh=mesh,
        in_specs=placed,
        out_specs=(P(), P("ens", "grid", None), P("grid", None)),
        check_vma=False,
    )
```

time: 80.1 us -> 63.1 us (0.79)
  local copies, waits for them, and re-layouts: 15.2 us -> 0 us
  between operations: 2.4 us -> 0.64 us
    unnamed x10 -> x0, local copies, waits for them, and re-layouts: 15.2 us -> none
    pallas_call x1 -> x2, Pallas kernels: 62.1 us -> 62.3 us  [the longest x1 56.3 us: per_device(): pl.pallas_call(functools.partial(kernel, sizes), out_shape=(pltpu.VMEM((1...]
where the time goes in v2:
time: 63.1 us; the launch traced here: 62.9 us
  Pallas kernels  62.3 us (99%)
  between operations  0.64 us (1%)
    pallas_call x1, Pallas kernels, per_device(): pl.pallas_call(functools.partial(kernel, sizes), out_shape=(pltpu.VMEM((1...  56.3 us
    pallas_call x1, Pallas kernels, per_device(): pl.pallas_call(copy_out, out_shape=out_shape, in_specs=[vmem, vmem, vmem]...  6.04 us

profile of v2, /device:TPU:1, one launch (start us, length us, event | category | flops | bytes accessed | tf_op | source)
XLA Modules:
  0.0 62.9 jit_solution(2349572069512096176)
XLA Ops:
  0.6 56.3 %crps_step.1 = (bf16[1,6144,1024]{2,1,0:T(8,128)(2,1)S(1)}, f32[64,100]{1,0:T(8,128)S(1)}, f32[1,1]{1,0:T(1,128)}) custom-call(bf16[1,6144,1024]{2,1,0:T(8,128)(2,1)} %latent_hbm.1, bf16[100,1024]{1,0:T(8,128)(2,1)} %bitcast.4, f32[100,6144]{1,0:T(8,128)} %truth_hbm.1, f32[48,128]{1,0:T(8,128)} %bitcast.5, f32[1,100]{1,0:T(1,128)} %bitcast.6), custom_call_target="tpu_custom_call" | custom-call | tf_op jit(solution)/shard_map/crps_step/pallas_call | solution.py:405
  56.9 6.0 %copy_out.1 = (bf16[1,6144,1024]{2,1,0:T(8,128)(2,1)}, f32[64,100]{1,0:T(8,128)}, f32[1,1]{1,0:T(1,128)}) custom-call(bf16[1,6144,1024]{2,1,0:T(8,128)(2,1)S(1)} %get-tuple-element.9.latent_grad, f32[64,100]{1,0:T(8,128)S(1)} %get-tuple-element.10.wgrad, f32[1,1]{1,0:T(1,128)} %get-tuple-element.11.loss), custom_call_target="tpu_custom_call" | custom-call | tf_op jit(solution)/shard_map/copy_out/pallas_call | solution.py:459

commit v3 on v2

--- a/solution.py
+++ b/solution.py
@@ -52,8 +52,7 @@
     area_hbm,
     var_hbm,
     out_ref,
-    wgrad_ref,
-    loss_ref,
+    summed_ref,
     latent,
     weight_in,
     weight,
@@ -73,6 +72,7 @@
     brecv,
     crecv,
     load_sem,
+    first_sem,
     truth_sem,
     small_sem,
     psend_sem,
@@ -97,51 +97,69 @@
     tail = blocks * whole
     me = lax.axis_index("ens")
     mine = lax.axis_index("grid")
-    my_y, my_z = me // half, me % half
-    core, spot = mine % 2, mine // 2
+    my_y, my_z = lax.div(me, half), lax.rem(me, half)
+    core, spot = lax.rem(mine, 2), lax.div(mine, 2)
     spots = shards // 2
     place = my_y * spots + spot
     places = 2 * spots
 
+    def member(slot, way):
+        y, z = (slot // half, slot % half) if isinstance(slot, int) else (lax.div(slot, half), lax.rem(slot, half))
+        return lax.rem(my_y + y, 2) * half + lax.rem(my_z + half + way * z, half)
+
     def sent_to(slot):
-        return ((my_y + slot // half) % 2) * half + (my_z + slot % half) % half
+        return member(slot, 1)
 
     def came_from(slot):
-        return ((my_y + slot // half) % 2) * half + (my_z + half - slot % half) % half
+        return member(slot, -1)
+
+    def turn(step):
+        if isinstance(step, int):
+            return (1 - step % 2) * half + (2, 3, 1, 0)[step // 2]
+        pair = lax.div(step, 2)
+        return (1 - lax.rem(step, 2)) * half + 2 + pair - lax.div(pair, 2) * (2 * pair - 1)
 
     def device_at(there):
-        return {"ens": there // spots * half + my_z, "grid": there % spots * 2 + core}
+        y, there = there
+        return {"ens": y * half + my_z, "grid": there * 2 + core}
+
+    def partner(step):
+        far = (2, 1, 3, 0)
+        x = lax.rem(lax.rem(spot, 4) + far[(step - 1) // 4], 4)
+        y = lax.rem(lax.div(spot, 4) * 2 + my_y + far[(step - 1) % 4], 4)
+        return lax.rem(y, 2), lax.div(y, 2) * 4 + x
 
     def load(c):
         rows = pl.ds(c * chunk, chunk)
         return pltpu.make_async_copy(latent_hbm.at[0, rows], latent.at[rows], load_sem.at[c])
 
+    def load_first(slot):
+        rows = pl.ds(pl.multiple_of(sent_to(slot) * width, LANES), width)
+        return pltpu.make_async_copy(latent_hbm.at[0, rows], latent.at[rows], first_sem.at[slot])
+
     def load_truth(c):
         first = pl.multiple_of(c * chunk + me * width, LANES)
         return pltpu.make_async_copy(truth_hbm.at[:, pl.ds(first, width)], truth.at[c], truth_sem.at[c])
+
+    sibling = mine + 1 - 2 * core
+    barrier = pltpu.get_barrier_semaphore()
+    for slot in range(1, count):
+        pl.semaphore_signal(barrier, inc=1, device_id={"ens": sent_to(slot)}, device_id_type=MESH)
+    for step in range(1, places):
+        pl.semaphore_signal(barrier, inc=1, device_id=device_at(partner(step)), device_id_type=MESH)
+    pl.semaphore_signal(barrier, inc=1, device_id={"grid": sibling}, device_id_type=MESH)
 
     small = [
         pltpu.make_async_copy(weight_hbm, weight_in, small_sem.at[0]),
         pltpu.make_async_copy(var_hbm, var_in, small_sem.at[1]),
         pltpu.make_async_copy(area_hbm, area, small_sem.at[2]),
     ]
-    for copy in small:
+    small[0].start()
+    for step in range(count):
+        load_first(turn(step)).start()
+    for copy in small[1:]:
         copy.start()
-    for c in range(CHUNKS):
-        load(c).start()
-    for c in range(CHUNKS):
-        load_truth(c).start()
-
-    sibling = mine + 1 - 2 * core
-    barrier = pltpu.get_barrier_semaphore()
-    for slot in range(1, count):
-        pl.semaphore_signal(barrier, inc=1, device_id={"ens": sent_to(slot)}, device_id_type=MESH)
-    for step in range(1, places):
-        pl.semaphore_signal(barrier, inc=1, device_id=device_at((place + step) % places), device_id_type=MESH)
-    pl.semaphore_signal(barrier, inc=1, device_id={"grid": sibling}, device_id_type=MESH)
-
-    for copy in small:
-        copy.wait()
+    small[0].wait()
     weight[pl.ds(0, whole), :] = weight_in[pl.ds(0, whole), :]
     weight[pl.ds(whole, padded - whole), :] = jnp.concatenate(
         [
@@ -150,8 +168,6 @@
         ],
         axis=0,
     ).astype(jnp.bfloat16)
-    row = jnp.concatenate([var_in[...], jnp.zeros((1, LANES - nvar), jnp.float32)], axis=1)
-    var[...] = jnp.broadcast_to(row, (LANES, LANES)).T
 
     def send_preds(c, slot):
         return pltpu.make_async_remote_copy(
@@ -185,14 +201,14 @@
         )
 
     def send_share(step):
-        there = (place + step) % places
-        rows = pl.ds(pl.multiple_of(there // spots * brecv.shape[1], 8), brecv.shape[1])
+        y, there = partner(step)
+        rows = pl.ds(pl.multiple_of(y * brecv.shape[1], 8), brecv.shape[1])
         return pltpu.make_async_remote_copy(
-            src_ref=bsend.at[there % spots, rows],
+            src_ref=bsend.at[there, rows],
             dst_ref=brecv.at[place],
             send_sem=bsend_sem.at[step],
             recv_sem=brecv_sem.at[step],
-            device_id=device_at(there),
+            device_id=device_at((y, there)),
             device_id_type=MESH,
         )
 
@@ -221,29 +237,43 @@
         target[c, slot, pl.ds(tail, ROWS), :] = jnp.concatenate(rest, axis=0).astype(jnp.bfloat16)
 
     for c in range(CHUNKS):
-        load(c).wait()
+        if c > 0:
+            load(c).wait()
 
         def forward(step, carry, c=c):
-            slot = count - 1 - step
+            slot = turn(step)
+            if c == 0:
+                load_first(slot).wait()
             project(psend, c, slot)
             if c == 0:
 
                 @pl.when(step == 0)
                 def _():
                     pl.semaphore_wait(barrier, count - 1 + places - 1 + 1)
+                    for later in range(1, CHUNKS):
+                        load(later).start()
+                    for later in range(CHUNKS):
+                        load_truth(later).start()
 
             send_preds(c, slot).start()
             return carry
 
         lax.fori_loop(0, count - 1, forward, 0)
+        if c == 0:
+            load_first(0).wait()
         project(precv, c, 0)
+
+    for copy in small[1:]:
+        copy.wait()
+    row = jnp.concatenate([var_in[...], jnp.zeros((1, LANES - nvar), jnp.float32)], axis=1)
+    var[...] = jnp.broadcast_to(row, (LANES, LANES)).T
 
     total = jnp.zeros((8, LANES), jnp.float32)
     for c in range(CHUNKS):
         load_truth(c).wait()
         for slot in range(1, count):
             send_preds(c, slot).wait_recv()
-        first = (c * chunk + me * width) // LANES
+        first = c * chunk // LANES + me * blocks
 
         def put(rows, values, c=c):
             grecv[c, 0, rows, :] = values[0].astype(jnp.bfloat16)
@@ -251,9 +281,9 @@
                 gsend[c, s, rows, :] = values[s].astype(jnp.bfloat16)
 
         def whole_rows(step, acc, c=c, first=first, put=put):
-            block = step % blocks
+            block = lax.rem(step, blocks)
             lanes = pl.ds(pl.multiple_of(block * LANES, LANES), LANES)
-            start = pl.multiple_of(step // blocks * ROWS, ROWS)
+            start = pl.multiple_of(lax.div(step, blocks) * ROWS, ROWS)
             rows = pl.ds(pl.multiple_of(block * whole + start, ROWS), ROWS)
             members = [precv[c, s, rows, :].astype(jnp.float32) for s in range(count)]
             target = truth[c, pl.ds(start, ROWS), lanes]
@@ -277,15 +307,20 @@
         rest = jnp.zeros((ROWS - 8, LANES), jnp.float32)
         put(rows, [jnp.concatenate([value, rest], axis=0) for value in pulled])
         total = total + terms
-        for slot in range(count - 1, 0, -1):
-            send_grads(c, slot).start()
+        for step in range(count - 1):
+            send_grads(c, turn(step)).start()
     partial = jnp.sum(total)
 
     cut = 256
 
-    def weight_part(step, c):
+    def weight_part(step, c, first=0, length=chunk):
         lanes = pl.ds(pl.multiple_of(step * cut, cut), cut)
-        part = jnp.dot(grads[...], latent[pl.ds(c * chunk, chunk), lanes], preferred_element_type=jnp.float32)
+        first = pl.multiple_of(first, LANES)
+        part = jnp.dot(
+            grads[:, pl.ds(first, length)],
+            latent[pl.ds(pl.multiple_of(c * chunk + first, LANES), length), lanes],
+            preferred_element_type=jnp.float32,
+        )
         if c == 0:
             wsum[pl.ds(0, padded), lanes] = part
         else:
@@ -305,30 +340,37 @@
 
         lax.fori_loop(start, stop, step_of, 0)
 
-    for c in range(CHUNKS):
+    def unpack(slot, c):
+        at = sent_to(slot) * width
+        last = grecv[c, slot, pl.ds(tail, ROWS), :].astype(jnp.float32)
+        for b in range(blocks):
+            lanes = pl.ds(pl.multiple_of(at + b * LANES, LANES), LANES)
+            grads[pl.ds(0, whole), lanes] = grecv[c, slot, pl.ds(b * whole, whole), :]
+            grads[pl.ds(whole, ROWS), lanes] = jnp.concatenate(
+                [last[b * left : (b + 1) * left], jnp.zeros((ROWS - left, LANES), jnp.float32)], axis=0
+            ).astype(jnp.bfloat16)
+
+    for c in range(CHUNKS - 1):
         for slot in range(1, count):
             send_grads(c, slot).wait_recv()
-
-        def unpack(slot, c=c):
-            at = sent_to(slot) * width
-            last = grecv[c, slot, pl.ds(tail, ROWS), :].astype(jnp.float32)
-            for b in range(blocks):
-                lanes = pl.ds(pl.multiple_of(at + b * LANES, LANES), LANES)
-                grads[pl.ds(0, whole), lanes] = grecv[c, slot, pl.ds(b * whole, whole), :]
-                grads[pl.ds(whole, ROWS), lanes] = jnp.concatenate(
-                    [last[b * left : (b + 1) * left], jnp.zeros((ROWS - left, LANES), jnp.float32)], axis=0
-                ).astype(jnp.bfloat16)
-
-        loop(0, count, unpack)
-        if c < CHUNKS - 1:
-            loop(0, lat // cut, lambda step, c=c: weight_part(step, c))
-            loop(0, chunk // cut, lambda step, c=c: latent_part(step, c))
+        loop(0, count, lambda slot, c=c: unpack(slot, c))
+        loop(0, lat // cut, lambda step, c=c: weight_part(step, c))
+        loop(0, chunk // cut, lambda step, c=c: latent_part(step, c))
 
     c = CHUNKS - 1
+    side = half * width
+    for slot in range(half, count):
+        send_grads(c, slot).wait_recv()
+    loop(half, count, lambda slot: unpack(slot, c))
+    loop(0, lat // cut, lambda step: weight_part(step, c, (1 - my_y) * side, side))
+    for slot in range(1, half):
+        send_grads(c, slot).wait_recv()
+    loop(0, half, lambda slot: unpack(slot, c))
+
     wsum[pl.ds(padded, LANES - padded), :] = jnp.broadcast_to(partial, (LANES - padded, lat))
 
     def weight_sent(step):
-        weight_part(step, c)
+        weight_part(step, c, my_y * side, side)
         for b in range(cut // LANES):
             lanes = pl.ds(pl.multiple_of(step * cut + b * LANES, LANES), LANES)
             turned = wsum[:, lanes].T
@@ -337,15 +379,19 @@
         send_core(step).start()
 
     loop(0, lat // cut, weight_sent)
-    early = 2
-    loop(0, early, lambda step: latent_part(step, c))
     for step in range(lat // cut):
         send_core(step).wait_recv()
     bsend[...] = asend[core] + arecv[...]
     for step in range(1, places):
         send_share(step).start()
     brecv[place] = bsend[spot, pl.ds(pl.multiple_of(my_y * brecv.shape[1], 8), brecv.shape[1]), :]
-    loop(early, chunk // cut, lambda step: latent_part(step, c))
+    loop(0, chunk // cut, lambda step: latent_part(step, c))
+    for c in range(CHUNKS):
+        for slot in range(1, count):
+            send_preds(c, slot).wait_send()
+            send_grads(c, slot).wait_send()
+    for step in range(lat // cut):
+        send_core(step).wait_send()
     for step in range(1, places):
         send_share(step).wait_recv()
     summed = brecv[0]
@@ -354,35 +400,34 @@
     crecv[me] = summed
     for slot in range(1, count):
         send_sum(slot).start()
+    for step in range(1, places):
+        send_share(step).wait_send()
     for slot in range(1, count):
         send_sum(slot).wait_recv()
     for y in range(2):
         final = crecv[y * half]
         for k in range(1, half):
             final = final + crecv[y * half + k]
-        rows = pl.ds(y * brecv.shape[1], brecv.shape[1])
-        wgrad_ref[rows, :] = final[:, :nvar] * (1.0 / math.sqrt(points * shards * count))
-        if y == 0:
-            loss_ref[...] = final[0:1, LANES - 1 : LANES] * (1.0 / (points * shards * nvar))
-
-    for c in range(CHUNKS):
-        for slot in range(1, count):
-            send_preds(c, slot).wait_send()
-            send_grads(c, slot).wait_send()
-    for step in range(lat // cut):
-        send_core(step).wait_send()
-    for step in range(1, places):
-        send_share(step).wait_send()
+        summed_ref[pl.ds(y * brecv.shape[1], brecv.shape[1]), :] = final
+
     for slot in range(1, count):
         send_sum(slot).wait_send()
 
 
-def copy_out(latent_grad, wgrad, loss, latent_out, wgrad_out, loss_out, sem):
-    copy = pltpu.make_async_copy(latent_grad, latent_out, sem)
-    copy.start()
-    wgrad_out[...] = wgrad[...]
-    loss_out[...] = loss[...]
-    copy.wait()
+def copy_out(sizes, latent_grad, summed, latent_out, wgrad_out, loss_out, wgrad, loss, sem):
+    count, shards, points, lat, nvar = sizes
+    copies = [
+        pltpu.make_async_copy(latent_grad, latent_out, sem.at[0]),
+        pltpu.make_async_copy(wgrad, wgrad_out, sem.at[1]),
+        pltpu.make_async_copy(loss, loss_out, sem.at[2]),
+    ]
+    copies[0].start()
+    wgrad[...] = summed[:, :nvar] * (1.0 / math.sqrt(points * shards * count))
+    loss[...] = summed[0:1, LANES - 1 : LANES] * (1.0 / (points * shards * nvar))
+    for copy in copies[1:]:
+        copy.start()
+    for copy in copies:
+        copy.wait()
 
 
 def per_device(latent, proj_weight, truth, area_weight, var_weight):
@@ -402,11 +447,11 @@
         jax.ShapeDtypeStruct((share, nvar), jnp.float32),
         jax.ShapeDtypeStruct((1, 1), jnp.float32),
     )
-    results = pl.pallas_call(
+    latent_grad, summed = pl.pallas_call(
         functools.partial(kernel, sizes),
-        out_shape=(pltpu.VMEM((1, points, lat), jnp.bfloat16), *out_shape[1:]),
+        out_shape=(pltpu.VMEM((1, points, lat), jnp.bfloat16), pltpu.VMEM((share, LANES), jnp.float32)),
         in_specs=[hbm] * 5,
-        out_specs=(vmem, vmem, vmem),
+        out_specs=(vmem, vmem),
         scratch_shapes=[
             pltpu.VMEM((points, lat), jnp.bfloat16),
             pltpu.VMEM((nvar, lat), jnp.bfloat16),
@@ -427,6 +472,7 @@
             pltpu.VMEM((shards, share // 2, LANES), jnp.float32),
             pltpu.VMEM((count, share // 2, LANES), jnp.float32),
             dma((CHUNKS,)),
+            dma((count,)),
             dma((CHUNKS,)),
             dma((3,)),
             dma((CHUNKS, count)),
@@ -457,14 +503,18 @@
         )
     )
     latent_grad, weight_grad, loss = pl.pallas_call(
-        copy_out,
+        functools.partial(copy_out, sizes),
         out_shape=out_shape,
-        in_specs=[vmem, vmem, vmem],
-        out_specs=(hbm, vmem, vmem),
-        scratch_shapes=[dma],
+        in_specs=[vmem, vmem],
+        out_specs=(hbm, hbm, hbm),
+        scratch_shapes=[
+            pltpu.VMEM((share, nvar), jnp.float32),
+            pltpu.VMEM((1, 1), jnp.float32),
+            dma((3,)),
+        ],
         compiler_params=pltpu.CompilerParams(vmem_limit_bytes=2**20),
         name="copy_out",
-    )(pltpu.with_memory_space_constraint(results[0], pltpu.VMEM), *results[1:])
+    )(*(pltpu.with_memory_space_constraint(x, pltpu.VMEM) for x in (latent_grad, summed)))
     return (loss[0, 0], latent_grad, weight_grad)
 
 

time: 63.1 us -> 60.6 us (0.960)
  Pallas kernels: 62.3 us -> 59.8 us
    pallas_call x1, Pallas kernels: 56.3 us -> 55 us  [per_device(): pl.pallas_call(functools.partial(kernel, sizes), out_shape=(pltpu.VMEM((1...]
    pallas_call x1, Pallas kernels: 6.04 us -> 4.81 us  [per_device(): pl.pallas_call(functools.partial(copy_out, sizes), out_shape=out_shape, i...]
where the time goes in v3:
time: 60.6 us; the launch traced here: 60.5 us
  Pallas kernels  59.8 us (99%)
  between operations  0.64 us (1%)
    pallas_call x1, Pallas kernels, per_device(): pl.pallas_call(functools.partial(kernel, sizes), out_shape=(pltpu.VMEM((1...  55 us
    pallas_call x1, Pallas kernels, per_device(): pl.pallas_call(functools.partial(copy_out, sizes), out_shape=out_shape, i...  4.81 us

profile of v3, /device:TPU:1, one launch (start us, length us, event | category | flops | bytes accessed | tf_op | source)
XLA Modules:
  0.0 60.5 jit_solution(2325647316427269517)
XLA Ops:
  0.6 55.0 %crps_step.1 = (bf16[1,6144,1024]{2,1,0:T(8,128)(2,1)S(1)}, f32[64,128]{1,0:T(8,128)S(1)}) custom-call(bf16[1,6144,1024]{2,1,0:T(8,128)(2,1)} %latent_hbm.1, bf16[100,1024]{1,0:T(8,128)(2,1)} %bitcast.4, f32[100,6144]{1,0:T(8,128)} %truth_hbm.1, f32[48,128]{1,0:T(8,128)} %bitcast.5, f32[1,100]{1,0:T(1,128)} %bitcast.6), custom_call_target="tpu_custom_call" | custom-call | tf_op jit(solution)/shard_map/crps_step/pallas_call | solution.py:450
  55.7 4.8 %copy_out.1 = (bf16[1,6144,1024]{2,1,0:T(8,128)(2,1)}, f32[64,100]{1,0:T(8,128)}, f32[1,1]{1,0:T(1,128)}) custom-call(bf16[1,6144,1024]{2,1,0:T(8,128)(2,1)S(1)} %get-tuple-element.8.latent_grad, f32[64,128]{1,0:T(8,128)S(1)} %get-tuple-element.9.summed), custom_call_target="tpu_custom_call" | custom-call | tf_op jit(solution)/shard_map/copy_out/pallas_call | solution.py:505

commit v4 on v3

--- a/solution.py
+++ b/solution.py
@@ -100,7 +100,6 @@
     my_y, my_z = lax.div(me, half), lax.rem(me, half)
     core, spot = lax.rem(mine, 2), lax.div(mine, 2)
     spots = shards // 2
-    place = my_y * spots + spot
     places = 2 * spots
 
     def member(slot, way):
@@ -173,8 +172,8 @@
         return pltpu.make_async_remote_copy(
             src_ref=psend.at[c, slot],
             dst_ref=precv.at[c, slot],
-            send_sem=psend_sem.at[c, slot],
-            recv_sem=precv_sem.at[c, slot],
+            send_sem=psend_sem.at[c],
+            recv_sem=precv_sem.at[c],
             device_id={"ens": sent_to(slot)},
             device_id_type=MESH,
         )
@@ -183,8 +182,8 @@
         return pltpu.make_async_remote_copy(
             src_ref=gsend.at[c, slot],
             dst_ref=grecv.at[c, slot],
-            send_sem=gsend_sem.at[c, slot],
-            recv_sem=grecv_sem.at[c, slot],
+            send_sem=gsend_sem.at[c],
+            recv_sem=grecv_sem.at[c, lax.div(slot, half) if not isinstance(slot, int) else slot // half],
             device_id={"ens": came_from(slot)},
             device_id_type=MESH,
         )
@@ -194,8 +193,8 @@
         return pltpu.make_async_remote_copy(
             src_ref=asend.at[1 - core, some],
             dst_ref=arecv.at[some],
-            send_sem=asend_sem.at[step],
-            recv_sem=arecv_sem.at[step],
+            send_sem=asend_sem,
+            recv_sem=arecv_sem,
             device_id={"grid": sibling},
             device_id_type=MESH,
         )
@@ -205,22 +204,28 @@
         rows = pl.ds(pl.multiple_of(y * brecv.shape[1], 8), brecv.shape[1])
         return pltpu.make_async_remote_copy(
             src_ref=bsend.at[there, rows],
-            dst_ref=brecv.at[place],
-            send_sem=bsend_sem.at[step],
-            recv_sem=brecv_sem.at[step],
+            dst_ref=brecv.at[step - 1],
+            send_sem=bsend_sem,
+            recv_sem=brecv_sem,
             device_id=device_at((y, there)),
             device_id_type=MESH,
         )
 
     def send_sum(slot):
         return pltpu.make_async_remote_copy(
-            src_ref=crecv.at[me],
-            dst_ref=crecv.at[me],
-            send_sem=csend_sem.at[slot],
-            recv_sem=crecv_sem.at[slot],
+            src_ref=crecv.at[0],
+            dst_ref=crecv.at[slot],
+            send_sem=csend_sem,
+            recv_sem=crecv_sem,
             device_id={"ens": sent_to(slot)},
             device_id_type=MESH,
         )
+
+    def all_of(some, sem):
+        return pltpu.make_async_copy(some, some, sem)
+
+    def blocks_of(ref, c, start, stop, sem):
+        return all_of(ref.at[c, pl.ds(start, stop - start)], sem)
 
     def project(target, c, slot):
         first = pl.multiple_of(c * chunk + sent_to(slot) * width, LANES)
@@ -271,8 +276,7 @@
     total = jnp.zeros((8, LANES), jnp.float32)
     for c in range(CHUNKS):
         load_truth(c).wait()
-        for slot in range(1, count):
-            send_preds(c, slot).wait_recv()
+        blocks_of(precv, c, 1, count, precv_sem.at[c]).wait()
         first = c * chunk // LANES + me * blocks
 
         def put(rows, values, c=c):
@@ -351,20 +355,18 @@
             ).astype(jnp.bfloat16)
 
     for c in range(CHUNKS - 1):
-        for slot in range(1, count):
-            send_grads(c, slot).wait_recv()
+        blocks_of(grecv, c, half, count, grecv_sem.at[c, 1]).wait()
+        blocks_of(grecv, c, 1, half, grecv_sem.at[c, 0]).wait()
         loop(0, count, lambda slot, c=c: unpack(slot, c))
         loop(0, lat // cut, lambda step, c=c: weight_part(step, c))
         loop(0, chunk // cut, lambda step, c=c: latent_part(step, c))
 
     c = CHUNKS - 1
     side = half * width
-    for slot in range(half, count):
-        send_grads(c, slot).wait_recv()
+    blocks_of(grecv, c, half, count, grecv_sem.at[c, 1]).wait()
     loop(half, count, lambda slot: unpack(slot, c))
     loop(0, lat // cut, lambda step: weight_part(step, c, (1 - my_y) * side, side))
-    for slot in range(1, half):
-        send_grads(c, slot).wait_recv()
+    blocks_of(grecv, c, 1, half, grecv_sem.at[c, 0]).wait()
     loop(0, half, lambda slot: unpack(slot, c))
 
     wsum[pl.ds(padded, LANES - padded), :] = jnp.broadcast_to(partial, (LANES - padded, lat))
@@ -379,39 +381,42 @@
         send_core(step).start()
 
     loop(0, lat // cut, weight_sent)
-    for step in range(lat // cut):
-        send_core(step).wait_recv()
+    all_of(arecv, arecv_sem).wait()
     bsend[...] = asend[core] + arecv[...]
     for step in range(1, places):
         send_share(step).start()
-    brecv[place] = bsend[spot, pl.ds(pl.multiple_of(my_y * brecv.shape[1], 8), brecv.shape[1]), :]
+    brecv[places - 1] = bsend[spot, pl.ds(pl.multiple_of(my_y * brecv.shape[1], 8), brecv.shape[1]), :]
     loop(0, chunk // cut, lambda step: latent_part(step, c))
     for c in range(CHUNKS):
-        for slot in range(1, count):
-            send_preds(c, slot).wait_send()
-            send_grads(c, slot).wait_send()
-    for step in range(lat // cut):
-        send_core(step).wait_send()
-    for step in range(1, places):
-        send_share(step).wait_recv()
-    summed = brecv[0]
+        blocks_of(psend, c, 1, count, psend_sem.at[c]).wait()
+        blocks_of(gsend, c, 1, count, gsend_sem.at[c]).wait()
+    all_of(asend.at[1 - core], asend_sem).wait()
+    all_of(brecv.at[pl.ds(0, places - 1)], brecv_sem).wait()
+
+    def share_from(x, y):
+        ways = (
+            lax.rem(lax.rem(spot, 4) + 4 - x, 4),
+            lax.rem(lax.div(spot, 4) * 2 + my_y + 4 - y, 4),
+        )
+        x, y = ((1 - lax.div(d, 2)) * (3 - 2 * d) + lax.div(d, 2) * (2 * d - 4) for d in ways)
+        return brecv[x * 4 + y]
+
+    summed = share_from(0, 0)
     for k in range(1, places):
-        summed = summed + brecv[k]
-    crecv[me] = summed
+        summed = summed + share_from(k // 4, k % 4)
+    crecv[0] = summed
     for slot in range(1, count):
         send_sum(slot).start()
-    for step in range(1, places):
-        send_share(step).wait_send()
-    for slot in range(1, count):
-        send_sum(slot).wait_recv()
+    all_of(brecv.at[pl.ds(0, places - 1)], bsend_sem).wait()
+    all_of(crecv.at[pl.ds(1, count - 1)], crecv_sem).wait()
     for y in range(2):
-        final = crecv[y * half]
+        side_at = lax.rem(my_y + y, 2) * half
+        final = crecv[side_at + my_z]
         for k in range(1, half):
-            final = final + crecv[y * half + k]
+            final = final + crecv[side_at + lax.rem(my_z + half - k, half)]
         summed_ref[pl.ds(y * brecv.shape[1], brecv.shape[1]), :] = final
 
-    for slot in range(1, count):
-        send_sum(slot).wait_send()
+    all_of(crecv.at[pl.ds(1, count - 1)], csend_sem).wait()
 
 
 def copy_out(sizes, latent_grad, summed, latent_out, wgrad_out, loss_out, wgrad, loss, sem):
@@ -475,16 +480,16 @@
             dma((count,)),
             dma((CHUNKS,)),
             dma((3,)),
-            dma((CHUNKS, count)),
-            dma((CHUNKS, count)),
-            dma((CHUNKS, count)),
-            dma((CHUNKS, count)),
-            dma((lat // 256,)),
-            dma((lat // 256,)),
-            dma((shards,)),
-            dma((shards,)),
-            dma((count,)),
-            dma((count,)),
+            dma((CHUNKS,)),
+            dma((CHUNKS,)),
+            dma((CHUNKS,)),
+            dma((CHUNKS, 2)),
+            dma,
+            dma,
+            dma,
+            dma,
+            dma,
+            dma,
         ],
         compiler_params=pltpu.CompilerParams(
             collective_id=0, has_side_effects=True, vmem_limit_bytes=36 * 2**20

time: 60.6 us -> 59.9 us (0.988)
  Pallas kernels: 59.8 us -> 59.1 us
    pallas_call x1, Pallas kernels: 55 us -> 54.3 us  [per_device(): pl.pallas_call(functools.partial(kernel, sizes), out_shape=(pltpu.VMEM((1...]
where the time goes in v4:
time: 59.9 us; the launch traced here: 59.7 us
  Pallas kernels  59.1 us (99%)
  between operations  0.64 us (1%)
    pallas_call x1, Pallas kernels, per_device(): pl.pallas_call(functools.partial(kernel, sizes), out_shape=(pltpu.VMEM((1...  54.3 us
    pallas_call x1, Pallas kernels, per_device(): pl.pallas_call(functools.partial(copy_out, sizes), out_shape=out_shape, i...  4.81 us

profile of v4, /device:TPU:1, one launch (start us, length us, event | category | flops | bytes accessed | tf_op | source)
XLA Modules:
  0.0 59.7 jit_solution(8033045462987990038)
XLA Ops:
  0.6 54.3 %crps_step.1 = (bf16[1,6144,1024]{2,1,0:T(8,128)(2,1)S(1)}, f32[64,128]{1,0:T(8,128)S(1)}) custom-call(bf16[1,6144,1024]{2,1,0:T(8,128)(2,1)} %latent_hbm.1, bf16[100,1024]{1,0:T(8,128)(2,1)} %bitcast.4, f32[100,6144]{1,0:T(8,128)} %truth_hbm.1, f32[48,128]{1,0:T(8,128)} %bitcast.5, f32[1,100]{1,0:T(1,128)} %bitcast.6), custom_call_target="tpu_custom_call" | custom-call | tf_op jit(solution)/shard_map/crps_step/pallas_call | solution.py:455
  54.9 4.8 %copy_out.1 = (bf16[1,6144,1024]{2,1,0:T(8,128)(2,1)}, f32[64,100]{1,0:T(8,128)}, f32[1,1]{1,0:T(1,128)}) custom-call(bf16[1,6144,1024]{2,1,0:T(8,128)(2,1)S(1)} %get-tuple-element.8.latent_grad, f32[64,128]{1,0:T(8,128)S(1)} %get-tuple-element.9.summed), custom_call_target="tpu_custom_call" | custom-call | tf_op jit(solution)/shard_map/copy_out/pallas_call | solution.py:510

commit v5 on v4

--- a/solution.py
+++ b/solution.py
@@ -11,6 +11,7 @@
 DELTA = 0.05
 CHUNKS = 3
 LANES = 128
+ORDER = (3, 1, 2, 7, 5, 6, 4)
 ROWS = 16
 MESH = pl.DeviceIdType.MESH
 
@@ -112,12 +113,6 @@
     def came_from(slot):
         return member(slot, -1)
 
-    def turn(step):
-        if isinstance(step, int):
-            return (1 - step % 2) * half + (2, 3, 1, 0)[step // 2]
-        pair = lax.div(step, 2)
-        return (1 - lax.rem(step, 2)) * half + 2 + pair - lax.div(pair, 2) * (2 * pair - 1)
-
     def device_at(there):
         y, there = there
         return {"ens": y * half + my_z, "grid": there * 2 + core}
@@ -154,8 +149,8 @@
         pltpu.make_async_copy(area_hbm, area, small_sem.at[2]),
     ]
     small[0].start()
-    for step in range(count):
-        load_first(turn(step)).start()
+    for slot in (*ORDER, 0):
+        load_first(slot).start()
     for copy in small[1:]:
         copy.start()
     small[0].wait()
@@ -245,8 +240,8 @@
         if c > 0:
             load(c).wait()
 
-        def forward(step, carry, c=c):
-            slot = turn(step)
+        def forward(step, rest, c=c):
+            slot = lax.rem(rest, count)
             if c == 0:
                 load_first(slot).wait()
             project(psend, c, slot)
@@ -261,9 +256,9 @@
                         load_truth(later).start()
 
             send_preds(c, slot).start()
-            return carry
-
-        lax.fori_loop(0, count - 1, forward, 0)
+            return lax.div(rest, count)
+
+        lax.fori_loop(0, count - 1, forward, sum(slot * count**k for k, slot in enumerate(ORDER)))
         if c == 0:
             load_first(0).wait()
         project(precv, c, 0)
@@ -311,8 +306,8 @@
         rest = jnp.zeros((ROWS - 8, LANES), jnp.float32)
         put(rows, [jnp.concatenate([value, rest], axis=0) for value in pulled])
         total = total + terms
-        for step in range(count - 1):
-            send_grads(c, turn(step)).start()
+        for slot in ORDER:
+            send_grads(c, slot).start()
     partial = jnp.sum(total)
 
     cut = 256
@@ -363,16 +358,16 @@
 
     c = CHUNKS - 1
     side = half * width
+    blocks_of(grecv, c, 1, half, grecv_sem.at[c, 0]).wait()
+    loop(0, half, lambda slot: unpack(slot, c))
+    loop(0, lat // cut, lambda step: weight_part(step, c, my_y * side, side))
     blocks_of(grecv, c, half, count, grecv_sem.at[c, 1]).wait()
     loop(half, count, lambda slot: unpack(slot, c))
-    loop(0, lat // cut, lambda step: weight_part(step, c, (1 - my_y) * side, side))
-    blocks_of(grecv, c, 1, half, grecv_sem.at[c, 0]).wait()
-    loop(0, half, lambda slot: unpack(slot, c))
 
     wsum[pl.ds(padded, LANES - padded), :] = jnp.broadcast_to(partial, (LANES - padded, lat))
 
     def weight_sent(step):
-        weight_part(step, c, my_y * side, side)
+        weight_part(step, c, (1 - my_y) * side, side)
         for b in range(cut // LANES):
             lanes = pl.ds(pl.multiple_of(step * cut + b * LANES, LANES), LANES)
             turned = wsum[:, lanes].T

time: 59.9 us -> 57.6 us (0.962)
  Pallas kernels: 59.1 us -> 56.9 us
    pallas_call x1, Pallas kernels: 54.3 us -> 52.1 us  [per_device(): pl.pallas_call(functools.partial(kernel, sizes), out_shape=(pltpu.VMEM((1...]
where the time goes in v5:
time: 57.6 us; the launch traced here: 57.5 us
  Pallas kernels  56.9 us (99%)
  between operations  0.64 us (1%)
    pallas_call x1, Pallas kernels, per_device(): pl.pallas_call(functools.partial(kernel, sizes), out_shape=(pltpu.VMEM((1...  52.1 us
    pallas_call x1, Pallas kernels, per_device(): pl.pallas_call(functools.partial(copy_out, sizes), out_shape=out_shape, i...  4.81 us

profile of v5, /device:TPU:1, one launch (start us, length us, event | category | flops | bytes accessed | tf_op | source)
XLA Modules:
  0.0 57.5 jit_solution(14868069101904112989)
XLA Ops:
  0.6 52.1 %crps_step.1 = (bf16[1,6144,1024]{2,1,0:T(8,128)(2,1)S(1)}, f32[64,128]{1,0:T(8,128)S(1)}) custom-call(bf16[1,6144,1024]{2,1,0:T(8,128)(2,1)} %latent_hbm.1, bf16[100,1024]{1,0:T(8,128)(2,1)} %bitcast.4, f32[100,6144]{1,0:T(8,128)} %truth_hbm.1, f32[48,128]{1,0:T(8,128)} %bitcast.5, f32[1,100]{1,0:T(1,128)} %bitcast.6), custom_call_target="tpu_custom_call" | custom-call | tf_op jit(solution)/shard_map/crps_step/pallas_call | solution.py:450
  52.7 4.8 %copy_out.1 = (bf16[1,6144,1024]{2,1,0:T(8,128)(2,1)}, f32[64,100]{1,0:T(8,128)}, f32[1,1]{1,0:T(1,128)}) custom-call(bf16[1,6144,1024]{2,1,0:T(8,128)(2,1)S(1)} %get-tuple-element.8.latent_grad, f32[64,128]{1,0:T(8,128)S(1)} %get-tuple-element.9.summed), custom_call_target="tpu_custom_call" | custom-call | tf_op jit(solution)/shard_map/copy_out/pallas_call | solution.py:505

commit v6 on v5

--- a/solution.py
+++ b/solution.py
@@ -316,7 +316,7 @@
         lanes = pl.ds(pl.multiple_of(step * cut, cut), cut)
         first = pl.multiple_of(first, LANES)
         part = jnp.dot(
-            grads[:, pl.ds(first, length)],
+            grads[c, :, pl.ds(first, length)],
             latent[pl.ds(pl.multiple_of(c * chunk + first, LANES), length), lanes],
             preferred_element_type=jnp.float32,
         )
@@ -329,7 +329,7 @@
         lanes = pl.ds(pl.multiple_of(step * cut, cut), cut)
         rows = pl.ds(pl.multiple_of(c * chunk + step * cut, cut), cut)
         out_ref[0, rows, :] = lax.dot_general(
-            grads[:, lanes], weight[...], (((0,), (0,)), ((), ())), preferred_element_type=jnp.float32
+            grads[c, :, lanes], weight[...], (((0,), (0,)), ((), ())), preferred_element_type=jnp.float32
         ).astype(jnp.bfloat16)
 
     def loop(start, stop, body):
@@ -344,8 +344,8 @@
         last = grecv[c, slot, pl.ds(tail, ROWS), :].astype(jnp.float32)
         for b in range(blocks):
             lanes = pl.ds(pl.multiple_of(at + b * LANES, LANES), LANES)
-            grads[pl.ds(0, whole), lanes] = grecv[c, slot, pl.ds(b * whole, whole), :]
-            grads[pl.ds(whole, ROWS), lanes] = jnp.concatenate(
+            grads[c, pl.ds(0, whole), lanes] = grecv[c, slot, pl.ds(b * whole, whole), :]
+            grads[c, pl.ds(whole, ROWS), lanes] = jnp.concatenate(
                 [last[b * left : (b + 1) * left], jnp.zeros((ROWS - left, LANES), jnp.float32)], axis=0
             ).astype(jnp.bfloat16)
 
@@ -354,7 +354,8 @@
         blocks_of(grecv, c, 1, half, grecv_sem.at[c, 0]).wait()
         loop(0, count, lambda slot, c=c: unpack(slot, c))
         loop(0, lat // cut, lambda step, c=c: weight_part(step, c))
-        loop(0, chunk // cut, lambda step, c=c: latent_part(step, c))
+        if c < CHUNKS - 2:
+            loop(0, chunk // cut, lambda step, c=c: latent_part(step, c))
 
     c = CHUNKS - 1
     side = half * width
@@ -382,6 +383,7 @@
         send_share(step).start()
     brecv[places - 1] = bsend[spot, pl.ds(pl.multiple_of(my_y * brecv.shape[1], 8), brecv.shape[1]), :]
     loop(0, chunk // cut, lambda step: latent_part(step, c))
+    loop(0, 4, lambda step: latent_part(step, c - 1))
     for c in range(CHUNKS):
         blocks_of(psend, c, 1, count, psend_sem.at[c]).wait()
         blocks_of(gsend, c, 1, count, gsend_sem.at[c]).wait()
@@ -402,6 +404,7 @@
     crecv[0] = summed
     for slot in range(1, count):
         send_sum(slot).start()
+    loop(4, chunk // cut, lambda step: latent_part(step, c - 1))
     all_of(brecv.at[pl.ds(0, places - 1)], bsend_sem).wait()
     all_of(crecv.at[pl.ds(1, count - 1)], crecv_sem).wait()
     for y in range(2):
@@ -464,7 +467,7 @@
             pltpu.VMEM((CHUNKS, count, packed, LANES), jnp.bfloat16),
             pltpu.VMEM((CHUNKS, count, packed, LANES), jnp.bfloat16),
             pltpu.VMEM((CHUNKS, count, packed, LANES), jnp.bfloat16),
-            pltpu.VMEM((padded, points // CHUNKS), jnp.bfloat16),
+            pltpu.VMEM((CHUNKS, padded, points // CHUNKS), jnp.bfloat16),
             pltpu.VMEM((LANES, lat), jnp.float32),
             pltpu.VMEM((2, shards // 2, share, LANES), jnp.float32),
             pltpu.VMEM((shards // 2, share, LANES), jnp.float32),

time: 57.6 us -> 56.6 us (0.983)
  Pallas kernels: 56.9 us -> 55.9 us
    pallas_call x1, Pallas kernels: 52.1 us -> 51.1 us  [per_device(): pl.pallas_call(functools.partial(kernel, sizes), out_shape=(pltpu.VMEM((1...]
where the time goes in v6:
time: 56.6 us; the launch traced here: 56.5 us
  Pallas kernels  55.9 us (99%)
  between operations  0.64 us (1%)
    pallas_call x1, Pallas kernels, per_device(): pl.pallas_call(functools.partial(kernel, sizes), out_shape=(pltpu.VMEM((1...  51.1 us
    pallas_call x1, Pallas kernels, per_device(): pl.pallas_call(functools.partial(copy_out, sizes), out_shape=out_shape, i...  4.81 us

profile of v6, /device:TPU:1, one launch (start us, length us, event | category | flops | bytes accessed | tf_op | source)
XLA Modules:
  0.0 56.5 jit_solution(9008779758001086596)
XLA Ops:
  0.6 51.1 %crps_step.1 = (bf16[1,6144,1024]{2,1,0:T(8,128)(2,1)S(1)}, f32[64,128]{1,0:T(8,128)S(1)}) custom-call(bf16[1,6144,1024]{2,1,0:T(8,128)(2,1)} %latent_hbm.1, bf16[100,1024]{1,0:T(8,128)(2,1)} %bitcast.4, f32[100,6144]{1,0:T(8,128)} %truth_hbm.1, f32[48,128]{1,0:T(8,128)} %bitcast.5, f32[1,100]{1,0:T(1,128)} %bitcast.6), custom_call_target="tpu_custom_call" | custom-call | tf_op jit(solution)/shard_map/crps_step/pallas_call | solution.py:453
  51.7 4.8 %copy_out.1 = (bf16[1,6144,1024]{2,1,0:T(8,128)(2,1)}, f32[64,100]{1,0:T(8,128)}, f32[1,1]{1,0:T(1,128)}) custom-call(bf16[1,6144,1024]{2,1,0:T(8,128)(2,1)S(1)} %get-tuple-element.8.latent_grad, f32[64,128]{1,0:T(8,128)S(1)} %get-tuple-element.9.summed), custom_call_target="tpu_custom_call" | custom-call | tf_op jit(solution)/shard_map/copy_out/pallas_call | solution.py:508

commit v7 on v6

--- a/solution.py
+++ b/solution.py
@@ -402,7 +402,7 @@
     for k in range(1, places):
         summed = summed + share_from(k // 4, k % 4)
     crecv[0] = summed
-    for slot in range(1, count):
+    for slot in (6, 5, 7, 2, 4, 1, 3):
         send_sum(slot).start()
     loop(4, chunk // cut, lambda step: latent_part(step, c - 1))
     all_of(brecv.at[pl.ds(0, places - 1)], bsend_sem).wait()

time: 56.6 us -> 56.6 us (level)
  no operation moved by 1% of the time
where the time goes in v7:
time: 56.6 us; the launch traced here: 56.5 us
  Pallas kernels  55.9 us (99%)
  between operations  0.64 us (1%)
    pallas_call x1, Pallas kernels, per_device(): pl.pallas_call(functools.partial(kernel, sizes), out_shape=(pltpu.VMEM((1...  51.1 us
    pallas_call x1, Pallas kernels, per_device(): pl.pallas_call(functools.partial(copy_out, sizes), out_shape=out_shape, i...  4.81 us

profile of v7, /device:TPU:1, one launch (start us, length us, event | category | flops | bytes accessed | tf_op | source)
XLA Modules:
  0.0 56.5 jit_solution(16824597746565313663)
XLA Ops:
  0.6 51.1 %crps_step.1 = (bf16[1,6144,1024]{2,1,0:T(8,128)(2,1)S(1)}, f32[64,128]{1,0:T(8,128)S(1)}) custom-call(bf16[1,6144,1024]{2,1,0:T(8,128)(2,1)} %latent_hbm.1, bf16[100,1024]{1,0:T(8,128)(2,1)} %bitcast.4, f32[100,6144]{1,0:T(8,128)} %truth_hbm.1, f32[48,128]{1,0:T(8,128)} %bitcast.5, f32[1,100]{1,0:T(1,128)} %bitcast.6), custom_call_target="tpu_custom_call" | custom-call | tf_op jit(solution)/shard_map/crps_step/pallas_call | solution.py:453
  51.7 4.8 %copy_out.1 = (bf16[1,6144,1024]{2,1,0:T(8,128)(2,1)}, f32[64,100]{1,0:T(8,128)}, f32[1,1]{1,0:T(1,128)}) custom-call(bf16[1,6144,1024]{2,1,0:T(8,128)(2,1)S(1)} %get-tuple-element.8.latent_grad, f32[64,128]{1,0:T(8,128)S(1)} %get-tuple-element.9.summed), custom_call_target="tpu_custom_call" | custom-call | tf_op jit(solution)/shard_map/copy_out/pallas_call | solution.py:508

commit v8 on v6

--- a/solution.py
+++ b/solution.py
@@ -368,10 +368,16 @@
     wsum[pl.ds(padded, LANES - padded), :] = jnp.broadcast_to(partial, (LANES - padded, lat))
 
     def weight_sent(step):
-        weight_part(step, c, (1 - my_y) * side, side)
+        lanes = pl.ds(pl.multiple_of(step * cut, cut), cut)
+        first = pl.multiple_of((1 - my_y) * side, LANES)
+        part = jnp.dot(
+            grads[c, :, pl.ds(first, side)],
+            latent[pl.ds(pl.multiple_of(c * chunk + first, LANES), side), lanes],
+            preferred_element_type=jnp.float32,
+        )
+        part = jnp.concatenate([wsum[pl.ds(0, padded), lanes] + part, wsum[pl.ds(padded, LANES - padded), lanes]], axis=0)
         for b in range(cut // LANES):
-            lanes = pl.ds(pl.multiple_of(step * cut + b * LANES, LANES), LANES)
-            turned = wsum[:, lanes].T
+            turned = part[:, b * LANES : (b + 1) * LANES].T
             asend[0, step * 2 + b] = turned[: LANES // 2]
             asend[1, step * 2 + b] = turned[LANES // 2 :]
         send_core(step).start()

time: 56.6 us -> 56.5 us (level)
  no operation moved by 1% of the time
where the time goes in v8:
time: 56.5 us; the launch traced here: 56.4 us
  Pallas kernels  55.8 us (99%)
  between operations  0.64 us (1%)
    pallas_call x1, Pallas kernels, per_device(): pl.pallas_call(functools.partial(kernel, sizes), out_shape=(pltpu.VMEM((1...  51 us
    pallas_call x1, Pallas kernels, per_device(): pl.pallas_call(functools.partial(copy_out, sizes), out_shape=out_shape, i...  4.81 us

profile of v8, /device:TPU:1, one launch (start us, length us, event | category | flops | bytes accessed | tf_op | source)
XLA Modules:
  0.0 56.4 jit_solution(2407181521800637912)
XLA Ops:
  0.6 51.0 %crps_step.1 = (bf16[1,6144,1024]{2,1,0:T(8,128)(2,1)S(1)}, f32[64,128]{1,0:T(8,128)S(1)}) custom-call(bf16[1,6144,1024]{2,1,0:T(8,128)(2,1)} %latent_hbm.1, bf16[100,1024]{1,0:T(8,128)(2,1)} %bitcast.4, f32[100,6144]{1,0:T(8,128)} %truth_hbm.1, f32[48,128]{1,0:T(8,128)} %bitcast.5, f32[1,100]{1,0:T(1,128)} %bitcast.6), custom_call_target="tpu_custom_call" | custom-call | tf_op jit(solution)/shard_map/crps_step/pallas_call | solution.py:459
  51.6 4.8 %copy_out.1 = (bf16[1,6144,1024]{2,1,0:T(8,128)(2,1)}, f32[64,100]{1,0:T(8,128)}, f32[1,1]{1,0:T(1,128)}) custom-call(bf16[1,6144,1024]{2,1,0:T(8,128)(2,1)S(1)} %get-tuple-element.8.latent_grad, f32[64,128]{1,0:T(8,128)S(1)} %get-tuple-element.9.summed), custom_call_target="tpu_custom_call" | custom-call | tf_op jit(solution)/shard_map/copy_out/pallas_call | solution.py:514
